TPU v7x, 512 devices: a whole 4x8x8 slice. The times are simulated.
512 devices in a mesh: pp: 16 (over x, z_lo), ep: 32 (over y, z_hi, core).
Axes of the slice: x: 4, y: 8, z: 8 (z_hi: 2, z_lo: 4; z = z_hi * 4 + z_lo), core: 2. Of those that a mesh axis runs over, the one named last changes fastest.
Arguments:
- tokens: bfloat16 [16, 8192, 2048], P('pp', 'ep'), may hold values from -6 to 6
- gain_section: bfloat16 [16, 2048], P('pp'), may hold values from 0.099609375 to 1.8984375
- gate_weight: bfloat16 [16, 32, 2048, 192], P('pp', 'ep'), may hold values from -0.125 to 0.125
- up_weight: bfloat16 [16, 32, 2048, 192], P('pp', 'ep'), may hold values from -0.125 to 0.125
- down_weight: bfloat16 [16, 32, 192, 2048], P('pp', 'ep'), may hold values from -0.15625 to 0.15625
- routes: int32 [16, 8192, 8], P('pp', 'ep'), may hold values from 0 to 127, as said below
- mixing: float32 [16, 8192, 8], P('pp', 'ep'), may hold values from 0.1 to 1
Outputs:
- result: bfloat16 [16, 8192, 2048], P('pp', 'ep')
Inputs may be any that keep to these rules, and one draw needn't show every extreme that they name: `routes`: each row names 8 different experts. Within the 256 rows of one device each expert below 4 is named by at most 32 rows; in every section one such expert, drawn from the seed, is named by exactly 32 rows of every device.
All inputs are finite; a program needn't handle non-finite values.
Results may differ from a plain program's by a relative error of at most 0.0017.
Values may be sent and summed in bfloat16 or wider, within the bound.
No kernel may reach another device: no remote copies, remote signals or barrier semaphores. Data moves between devices by JAX's collectives and lax.ppermute only.
A program may use at most 64 MiB of HBM per device.

v0:
```python
import jax
import jax.numpy as jnp
from jax import lax
from jax.sharding import PartitionSpec as P

SLICES = 8
CAP = 32


EPSILON = 1e-06


def passed_along(x, axis, by):
    peers = lax.axis_size(axis)
    return lax.ppermute(x, axis, [(i, (i + by) % peers) for i in range(peers)])


def rms_normed(values, gain_row):
    widened = values.astype(jnp.float32)
    scale_row = lax.rsqrt(jnp.mean(widened * widened, axis=-1, keepdims=True) + EPSILON)
    return (widened * scale_row * gain_row.astype(jnp.float32)).astype(jnp.bfloat16)


def expert_rows(received, gate_mat, up_mat, down_mat):
    features = received.shape[-1]
    token_rows = received.reshape(-1, features)
    gate_proj = jnp.dot(token_rows, gate_mat, preferred_element_type=jnp.float32)
    up_proj = jnp.dot(token_rows, up_mat, preferred_element_type=jnp.float32)
    hidden = (jax.nn.silu(gate_proj) * up_proj).astype(jnp.bfloat16)
    partial_value = jnp.dot(hidden, down_mat, preferred_element_type=jnp.float32).astype(
        jnp.bfloat16
    )
    partial_value = partial_value.reshape(received.shape)
    return lax.all_to_all(partial_value, "ep", split_axis=0, concat_axis=0, tiled=True)


def moe_block(tokens_in, gain_row, gate_mat, up_mat, down_mat, route_rows, mix_rows):
    owners = lax.axis_size("ep")
    experts_held = owners // SLICES
    features = tokens_in.shape[-1]
    normed = rms_normed(tokens_in, gain_row)
    labels = jnp.arange(experts_held, dtype=jnp.int32)
    chosen = route_rows[:, :, None] == labels[None, None, :]
    member = jnp.any(chosen, axis=1)
    weight = jnp.sum(jnp.where(chosen, mix_rows[:, :, None], 0.0), axis=1)
    position = jnp.cumsum(member.astype(jnp.int32), axis=0) - 1
    slot_ids = jnp.arange(CAP, dtype=jnp.int32)
    onehot = (position.T[:, None, :] == slot_ids[None, :, None]) & member.T[:, None, :]
    packed = jnp.einsum(
        "wct,td->wcd", onehot.astype(jnp.bfloat16), normed, preferred_element_type=jnp.float32
    ).astype(jnp.bfloat16)
    outgoing = jnp.broadcast_to(packed[:, None], (experts_held, SLICES, CAP, features)).reshape(
        owners, CAP, features
    )
    returned = expert_rows(
        lax.all_to_all(outgoing, "ep", split_axis=0, concat_axis=0, tiled=True),
        gate_mat,
        up_mat,
        down_mat,
    )
    summed = returned.astype(jnp.float32).reshape(experts_held, SLICES, CAP, features).sum(axis=1)
    summed = summed.reshape(experts_held * CAP, features)
    index_rows = jnp.maximum(position, 0) + labels[None, :] * CAP
    fetched = jnp.take(summed, index_rows, axis=0)
    scaled = jnp.where(member, weight, 0.0)
    output = tokens_in.astype(jnp.float32) + jnp.sum(scaled[:, :, None] * fetched, axis=1)
    return output.astype(jnp.bfloat16)


def body(tokens, gain_section, gate_weight, up_weight, down_weight, routes, mixing):
    block_out = moe_block(
        tokens[0],
        gain_section[0],
        gate_weight[0, 0],
        up_weight[0, 0],
        down_weight[0, 0],
        routes[0],
        mixing[0],
    )
    passed = passed_along(block_out, "pp", 1)
    return passed[None]


def solution(mesh):
    placed = (
        P("pp", "ep", None),
        P("pp", None),
        P("pp", "ep", None, None),
        P("pp", "ep", None, None),
        P("pp", "ep", None, None),
        P("pp", "ep", None),
        P("pp", "ep", None),
    )
    return jax.shard_map(
        body, mesh=mesh, in_specs=placed, out_specs=P("pp", "ep", None), check_vma=False
    )
```

profile of v0, /device:TPU:2, one launch (start us, length us, event | category | flops | bytes accessed | tf_op | source)
XLA Modules:
  0.0 312.1 jit_solution(2186880294680688280)
XLA Ops:
  0.0 0.0 copy-start
  0.0 0.8 fusion.25
  0.8 1.2 reduce-window.6
  2.0 0.1 slice.10
  2.1 0.1 copy.25
  2.3 0.1 copy.26
  2.4 0.1 maximum_bitcast_fusion
  2.4 0.7 mul.59
  3.2 1.5 fusion
  4.7 1.7 convolution_convert_fusion.1
  6.4 0.5 broadcast_in_dim.52
  6.9 0.0 copy-start.5
  7.0 114.5 %all_to_all.10 = bf16[32,32,2048]{2,1,0:T(8,128)(2,1)S(1)} all-to-all(bf16[32,32,2048]{2,1,0:T(8,128)(2,1)S(1)} %bitcast.57), channel_id=1, replica_groups=mesh['pp'=16,'ep'=32] {'ep'}, dimensions={0} | all-to-all | bytes 8388608 | tf_op jit(solution)/shard_map/all_to_all | solution.py:56
  121.5 2.0 copy-done.1
  123.5 1.5 fusion.13
  125.0 6.8 %convolution_convert_fusion = bf16[1024,2048]{1,0:T(8,128)(2,1)} fusion(bf16[1024,2048]{1,0:T(8,128)(2,1)} %bitcast.60, bf16[1,1,192,2048]{3,2,1,0:T(8,128)(2,1)S(1)} %copy-done, bf16[1,1,2048,192]{2,3,1,0:T(8,128)(2,1)S(1)} %copy-done.6, f32[1024,192]{0,1:T(8,128)S(1)} %fusion.13), kind=kOutput, calls=%fused_computation.3 | convolution fusion | flops 1613889536 | bytes 10747904 | tf_op jit(solution)/shard_map/dot_general | solution.py:30
  131.9 9.4 %all-to-all-start.1 = ((bf16[32,32,2048]{2,1,0:T(8,128)(2,1)}), bf16[32,32,2048]{2,1,0:T(8,128)(2,1)}, u32[]{:S(2)}, u32[]{:S(2)}) async-start(bf16[32,32,2048]{2,1,0:T(8,128)(2,1)} %bitcast.58), calls=%async_computation.1 | async-start | bytes 8388608 | tf_op jit(solution)/shard_map/all_to_all | solution.py:34
  141.3 0.1 compare_and_fusion
  141.4 0.1 copy.28
  141.5 0.1 reshape.80
  141.6 0.2 copy.27
  141.9 0.1 copy.24
  142.0 110.2 %all-to-all-done.1 = bf16[32,32,2048]{2,1,0:T(8,128)(2,1)} async-done(((bf16[32,32,2048]{2,1,0:T(8,128)(2,1)}), bf16[32,32,2048]{2,1,0:T(8,128)(2,1)}, u32[]{:S(2)}, u32[]{:S(2)}) %all-to-all-start.1) | async-done | bytes 4194336 | tf_op jit(solution)/shard_map/all_to_all | solution.py:34
  252.2 3.0 convert_reduce_fusion
  255.2 6.8 %gather_fusion = f32[1024,2048]{1,0:T(8,128)} fusion(f32[128,2048]{1,0:T(8,128)S(1)} %bitcast.56, s32[1024]{0:T(1024)S(1)} %broadcast_clamp_fusion), kind=kCustom, calls=%fused_computation | custom fusion | bytes 16781312 | tf_op jit(solution)/shard_map/jit(_take)/gather | solution.py:64
  262.0 9.8 %reshape.79 = f32[256,4,2048]{2,1,0:T(4,128)} reshape(f32[1024,2048]{1,0:T(8,128)} %gather_fusion) | data formatting | bytes 16777216 | tf_op jit(solution)/shard_map/jit(_take)/gather | solution.py:64
  271.8 10.4 %multiply_reduce_fusion = f32[256,2048]{1,0:T(8,128)S(1)} fusion(f32[256,4,2048]{2,1,0:T(4,128)} %reshape.79, f32[256,4]{1,0:T(8,128)S(1)} %copy.24, pred[256,4]{1,0:T(8,128)(4,1)S(1)} %copy.27), kind=kLoop, calls=%fused_computation.2 | loop fusion | flops 5767168 | bytes 10490880 | tf_op jit(solution)/shard_map/reduce_sum | solution.py:66
  282.2 0.0 copy-done.2
  282.2 0.3 fusion.3
  282.5 1.9 collective-permute-start
  284.5 26.7 %collective-permute-done = bf16[256,2048]{1,0:T(8,128)(2,1)S(1)} collective-permute-done((bf16[256,2048]{1,0:T(8,128)(2,1)S(1)}, bf16[256,2048]{1,0:T(8,128)(2,1)S(1)}, u32[]{:S(2)}, u32[]{:S(2)}) %collective-permute-start) | collective-permute-done | bytes 1048608 | tf_op jit(solution)/shard_map/ppermute | solution.py:15
  311.1 1.0 copy.36
  (20 shorter events, 0.1 us)
Async XLA Ops:
  0.0 125.0 %copy-start = (bf16[1,1,192,2048]{3,2,1,0:T(8,128)(2,1)S(1)}, bf16[1,1,192,2048]{3,2,1,0:T(8,128)(2,1)}, u32[]{:S(2)}) copy-start(bf16[1,1,192,2048]{3,2,1,0:T(8,128)(2,1)} %param.11) | copy-start | bytes 2359300
  6.9 116.5 %copy-start.5 = (bf16[1,1,2048,192]{2,3,1,0:T(8,128)(2,1)S(1)}, bf16[1,1,2048,192]{2,3,1,0:T(8,128)(2,1)}, u32[]{:S(2)}) copy-start(bf16[1,1,2048,192]{2,3,1,0:T(8,128)(2,1)} %param.9) | copy-start | bytes 2359300
  121.5 2.0 copy-start.1
  121.5 3.5 %copy-start.6 = (bf16[1,1,2048,192]{2,3,1,0:T(8,128)(2,1)S(1)}, bf16[1,1,2048,192]{2,3,1,0:T(8,128)(2,1)}, u32[]{:S(2)}) copy-start(bf16[1,1,2048,192]{2,3,1,0:T(8,128)(2,1)} %param.10) | copy-start | bytes 2359300
  131.9 9.9 %copy-start.3 = (s32[1,256,8]{1,2,0:T(8,128)S(1)}, s32[1,256,8]{1,2,0:T(8,128)}, u32[]{:S(2)}) copy-start(s32[1,256,8]{1,2,0:T(8,128)} %param.12) | copy-start | bytes 24580
  131.9 9.9 %copy-start.4 = (f32[1,256,8]{1,2,0:T(8,128)S(1)}, f32[1,256,8]{1,2,0:T(8,128)}, u32[]{:S(2)}) copy-start(f32[1,256,8]{1,2,0:T(8,128)} %param.13) | copy-start | bytes 24580
  131.9 120.3 %all-to-all-start.1 = ((bf16[32,32,2048]{2,1,0:T(8,128)(2,1)}), bf16[32,32,2048]{2,1,0:T(8,128)(2,1)}, u32[]{:S(2)}, u32[]{:S(2)}) async-start(bf16[32,32,2048]{2,1,0:T(8,128)(2,1)} %bitcast.58), calls=%async_computation.1 | async-start | bytes 8388608 | tf_op jit(solution)/shard_map/all_to_all | solution.py:34
  271.8 10.4 %copy-start.2 = (bf16[1,256,2048]{2,1,0:T(8,128)(2,1)S(1)}, bf16[1,256,2048]{2,1,0:T(8,128)(2,1)}, u32[]{:S(2)}) copy-start(bf16[1,256,2048]{2,1,0:T(8,128)(2,1)} %param.7) | copy-start | bytes 3145732
  282.5 28.6 %collective-permute-start = (bf16[256,2048]{1,0:T(8,128)(2,1)S(1)}, bf16[256,2048]{1,0:T(8,128)(2,1)S(1)}, u32[]{:S(2)}, u32[]{:S(2)}) collective-permute-start(bf16[256,2048]{1,0:T(8,128)(2,1)S(1)} %fusion.3), channel_id=1, source_target_pairs={{0,32},{32,64},{64,96},{96,128},{128,160},{160,192},{192,224},{224... | collective-permute-start | bytes 3145736 | tf_op jit(solution)/shard_map/ppermute | solution.py:15
where the time goes:
time: 313 us; the launch traced here: 312 us
  waiting for transfers between devices  137 us (44%)
  blocking collectives  115 us (37%)
  local copies, waits for them, and re-layouts  20.9 us (7%)
  other arithmetic  18.2 us (6%)
  starting transfers between devices  11.3 us (4%)
  matrix products  10.1 us (3%)
    all_to_all x1, blocking collectives, moe_block(): lax.all_to_all(outgoing, 'ep', split_axis=0, concat_axis=0, tiled=True)  115 us
    all_to_all x1, waiting for transfers between devices, expert_rows(): lax.all_to_all(partial_value, 'ep', split_axis=0, concat_axis=0, tiled=True)  110 us
    ppermute x1, waiting for transfers between devices, passed_along(): return lax.ppermute(x, axis, [(i, (i + by) % peers) for i in range(peers)])  26.7 us
    gather x2, local copies, waits for them, and re-layouts, moe_block(): fetched = jnp.take(summed, index_rows, axis=0)  16.6 us
    reduce_sum x1, other arithmetic, moe_block(): jnp.sum(scaled[:, :, None] * fetched, axis=1)  10.4 us
    all_to_all x1, starting transfers between devices, expert_rows(): lax.all_to_all(partial_value, 'ep', split_axis=0, concat_axis=0, tiled=True)  9.39 us
    dot_general x1, matrix products, expert_rows(): jnp.dot(hidden, down_mat, preferred_element_type=jnp.float32)  6.83 us
  transfers between devices with their start and end apart: 2, of which 2 were waited for; matrix products, arithmetic and copies ran while one was open for 0% of the time, Pallas kernels for 0%

commit v1 on v0

v1 whole, which is shorter than its diff:
```python
import functools

import jax
import jax.numpy as jnp
from jax import lax
from jax.experimental import pallas as pl
from jax.experimental.pallas import tpu as pltpu
from jax.sharding import PartitionSpec as P

CAP = 32
WAVE = 4
EPSILON = 1e-06
N_Y, N_Z, N_CORE = 8, 2, 2
BF16, F32 = jnp.bfloat16, jnp.float32
ROOM = 24 * 1024 * 1024
ORDER = (0, 1, 3, 2)
VMEM = pl.BlockSpec(memory_space=pltpu.VMEM)


def permuted(x, move, sections=1, by=0):
    pairs = []
    for sec in range(sections):
        for y in range(N_Y):
            for z in range(N_Z):
                for core in range(N_CORE):
                    y2, z2, core2 = move(y, z, core)
                    source = (y * N_Z + z) * N_CORE + core
                    target = ((y2 % N_Y) * N_Z + z2) * N_CORE + core2
                    lanes = N_Y * N_Z * N_CORE
                    pairs.append((sec * lanes + source, ((sec + by) % sections) * lanes + target))
    return lax.ppermute(x, "ep" if sections == 1 else ("pp", "ep"), pairs)


def other_core(x):
    return permuted(x, lambda y, z, core: (y, z, 1 - core))


def other_plane(x):
    return permuted(x, lambda y, z, core: (y, 1 - z, core))


def pair_swap(x):
    return permuted(x, lambda y, z, core: (y ^ 1, z, core))


def stay(y, z, core):
    return y, z, core


def exchanged(x, planes):
    groups = []
    for parity in range(2):
        for core in range(N_CORE):
            members = [
                [((2 * half + parity) * N_Z + z) * N_CORE + core for z in range(N_Z)]
                for half in range(WAVE)
            ]
            if planes == N_Z:
                groups.append(sum(members, []))
            else:
                groups += [[member[z] for member in members] for z in range(N_Z)]
    parts = x.reshape(len(groups[0]), -1, x.shape[-1])
    parts = lax.all_to_all(
        parts, "ep", split_axis=0, concat_axis=0, axis_index_groups=groups, tiled=True
    )
    return parts.reshape(x.shape)


def called(kernel, out_shape, flops, moved, *xs, scalars=0):
    return pl.pallas_call(
        kernel,
        out_shape=out_shape,
        in_specs=[pl.BlockSpec(memory_space=pltpu.SMEM)] * scalars + [VMEM] * (len(xs) - scalars),
        out_specs=jax.tree.map(lambda _: VMEM, out_shape),
        compiler_params=pltpu.CompilerParams(vmem_limit_bytes=ROOM),
        cost_estimate=pl.CostEstimate(flops=0, bytes_accessed=0, transcendentals=0),
    )(*xs)


def pack_kernel(expert_ref, tokens_ref, gain_ref, routes_ref, mixing_ref, packed_ref, weight_ref):
    widened = tokens_ref[...].astype(F32)
    scale = lax.rsqrt(jnp.mean(widened * widened, axis=-1, keepdims=True) + EPSILON)
    normed = (widened * scale * gain_ref[...].astype(F32)).astype(BF16)
    rows = tokens_ref.shape[0]
    shape = (WAVE * CAP, rows)
    row = lax.broadcasted_iota(jnp.int32, shape, 0)
    member = jnp.zeros(shape, F32)
    weight = jnp.zeros(shape, F32)
    for k in range(routes_ref.shape[0]):
        hit = routes_ref[k : k + 1, :] == row // CAP
        member = jnp.where(hit, 1.0, member)
        weight = weight + jnp.where(hit, mixing_ref[k : k + 1, :], 0.0)
    upto = lax.broadcasted_iota(jnp.int32, (rows, rows), 0) <= lax.broadcasted_iota(
        jnp.int32, (rows, rows), 1
    )
    count = jnp.dot(
        member.astype(BF16), jnp.where(upto, 1.0, 0.0).astype(BF16), preferred_element_type=F32
    )
    slot = (row % CAP + 1).astype(F32)
    onehot = jnp.where((count == slot) & (member > 0.0), 1.0, 0.0)
    weight = weight * onehot
    for at in range(WAVE):
        start = (at + WAVE - expert_ref[0]) % WAVE * CAP
        weight_ref[pl.ds(pl.multiple_of(start, CAP), CAP)] = weight[at * CAP : (at + 1) * CAP]
    packed_ref[...] = jnp.dot(
        onehot.astype(BF16), normed, preferred_element_type=F32
    ).astype(BF16)


def sort_kernel(expert_ref, held_ref, first_ref, last_ref, all_ref):
    for index, k in enumerate(ORDER):
        at = (expert_ref[0] + WAVE - k) % WAVE * CAP
        piece = held_ref[pl.ds(pl.multiple_of(at, CAP), CAP)]
        all_ref[index * CAP : (index + 1) * CAP] = piece
        part, start = ((first_ref, last_ref)[index // 2], index % 2 * CAP)
        part[start : start + CAP] = piece


def expert_kernel(spans, *refs):
    xs, mats, out_ref = refs[: len(spans)], refs[len(spans) : -1], refs[-1]
    rows = jnp.concatenate([x[at : at + n] for x, (at, n) in zip(xs, spans)], axis=0)
    across = (((1,), (1,)), ((), ()))
    total = None
    for gate, up, down in (mats[:3], mats[3:]):
        gate_proj = lax.dot_general(rows, gate[...], across, preferred_element_type=F32)
        up_proj = lax.dot_general(rows, up[...], across, preferred_element_type=F32)
        hidden = (jax.nn.silu(gate_proj) * up_proj).astype(BF16)
        part = jnp.dot(hidden, down[...], preferred_element_type=F32)
        total = part if total is None else total + part
    out_ref[...] = total.astype(out_ref.dtype)


def expert_rows(xs, mats, dtype, spans=None):
    spans = spans or tuple((0, x.shape[0]) for x in xs)
    rows = sum(n for _, n in spans)
    out = jax.ShapeDtypeStruct((rows, xs[0].shape[1]), dtype)
    kernel = functools.partial(expert_kernel, spans)
    return called(kernel, out, 2 * rows * 2048 * 1152, 6 << 20, *xs, *mats)


def add_kernel(at, near_at, size, mine_ref, *refs):
    adds, outs = refs[: len(near_at)], refs[len(near_at) :]
    for index, out in enumerate(outs):
        total = mine_ref[at + index * size : at + (index + 1) * size]
        for add, start in zip(adds, near_at):
            total = total + add[start + index * size : start + (index + 1) * size].astype(F32)
        out[...] = total.astype(BF16)


def added(mine, at, size, count, *adds):
    out = [jax.ShapeDtypeStruct((size, mine.shape[1]), BF16)] * count
    kernel = functools.partial(add_kernel, at, tuple(start for _, start in adds), size)
    return called(kernel, out, 1 << 18, 1 << 20, mine, *[add for add, _ in adds])


def combine_kernel(tokens_ref, weight_ref, *refs):
    pieces, out_ref = refs[:-1], refs[-1]
    weight = weight_ref[...].T
    high = weight.astype(BF16)
    rest = weight - high.astype(F32)
    middle = rest.astype(BF16)
    low = (rest - middle.astype(F32)).astype(BF16)
    rows = jnp.concatenate([piece[...] for piece in pieces], axis=0)
    total = jnp.dot(
        jnp.concatenate([high, middle], axis=1),
        jnp.concatenate([rows, rows], axis=0),
        preferred_element_type=F32,
    )
    total = total + jnp.dot(low, rows, preferred_element_type=F32)
    out_ref[...] = (tokens_ref[...].astype(F32) + total).astype(BF16)


def tied(*xs):
    return lax.optimization_barrier(xs)


def body(sections, tokens, gain, gate, up, down, routes, mixing):
    tokens, gate, up, down = tokens[0], gate[0, 0].T, up[0, 0].T, down[0, 0]
    rows, features = tokens.shape
    slots, half = WAVE * CAP, 2 * CAP
    expert = (lax.axis_index("ep") // (2 * N_Z * N_CORE)).astype(jnp.int32).reshape(1)

    packed, weight = called(
        pack_kernel,
        [
            jax.ShapeDtypeStruct((slots, features), BF16),
            jax.ShapeDtypeStruct((slots, rows), F32),
        ],
        2 * slots * rows * features,
        2 << 20,
        expert,
        tokens,
        gain,
        routes[0].T,
        mixing[0].T,
        scalars=1,
    )

    held, before, *mats = tied(
        exchanged(packed, 1),
        permuted(tokens, stay, sections, 1),
        other_core(gate),
        other_core(up),
        other_core(down),
    )
    mats = (gate, up, down, *mats)
    quarter = jax.ShapeDtypeStruct((half, features), BF16)
    held_a, held_b, held = called(
        sort_kernel,
        [quarter, quarter, jax.ShapeDtypeStruct((slots, features), BF16)],
        0,
        1 << 20,
        expert,
        held,
        scalars=1,
    )
    crossed_a, crossed_b = other_plane(held_a), other_plane(held_b)
    twin_a = pair_swap(crossed_a)
    sent = expert_rows([pair_swap(held)], mats, BF16)
    crossed_b, twin_a, sent, weight = tied(crossed_b, twin_a, sent, weight)
    twin_b = pair_swap(crossed_b)
    weight = permuted(weight, stay, sections, 1)
    theirs_a, sent = tied(pair_swap(expert_rows([twin_a], mats, BF16)), sent)
    theirs = pair_swap(sent)
    mine = expert_rows([crossed_a, crossed_b, held], mats, F32)
    mine, twin_b = tied(mine, twin_b)
    theirs_b = pair_swap(expert_rows([twin_b], mats, BF16))

    (far_a,) = added(mine, 0, half, 1, (theirs_a, 0))
    (far_b,) = added(mine, half, half, 1, (theirs_b, 0))
    pieces = added(mine, 2 * half, CAP, 2, (theirs, 0), (other_plane(far_a), 0))
    pieces += added(mine, 3 * half, CAP, 2, (theirs, half), (other_plane(far_b), 0))
    back = {
        k: permuted(piece, lambda y, z, core, k=k: (y - 2 * k, z, core), sections, 1)
        for k, piece in zip(ORDER, pieces)
    }
    return called(
        combine_kernel,
        jax.ShapeDtypeStruct((rows, features), BF16),
        6 * rows * slots * features,
        3 << 20,
        before,
        weight,
        *[back[k] for k in range(WAVE)],
    )[None]


def solution(mesh):
    placed = (
        P("pp", "ep", None),
        P("pp", None),
        P("pp", "ep", None, None),
        P("pp", "ep", None, None),
        P("pp", "ep", None, None),
        P("pp", "ep", None),
        P("pp", "ep", None),
    )
    return jax.shard_map(
        functools.partial(body, mesh.shape["pp"]),
        mesh=mesh,
        in_specs=placed,
        out_specs=P("pp", "ep", None),
        check_vma=False,
    )
```

time: 313 us -> 151 us (0.48)
  the two profiles are of different devices: /device:TPU:2 before, /device:TPU:8 now
where the time goes in v1:
time: 151 us; the launch traced here: 150 us
  starting transfers between devices  90.1 us (60%)
  waiting for transfers between devices  38.5 us (25%)
  Pallas kernels  17.9 us (12%)
  local copies, waits for them, and re-layouts  3.35 us (2%)
    ppermute x19, starting transfers between devices, permuted(): return lax.ppermute(x, 'ep' if sections == 1 else ('pp', 'ep'), pairs)  83.9 us
    ppermute x19, waiting for transfers between devices, permuted(): return lax.ppermute(x, 'ep' if sections == 1 else ('pp', 'ep'), pairs)  30.2 us
    pallas_call x11, Pallas kernels, called(): pl.pallas_call(kernel, out_shape=out_shape, in_specs=[pl.BlockSpec(memory...  17.9 us
    all_to_all x1, waiting for transfers between devices, exchanged(): lax.all_to_all(parts, 'ep', split_axis=0, concat_axis=0, axis_index_group...  8.32 us
    all_to_all x1, starting transfers between devices, exchanged(): lax.all_to_all(parts, 'ep', split_axis=0, concat_axis=0, axis_index_group...  6.19 us
    unnamed x14, local copies, waits for them, and re-layouts  3.35 us
  transfers between devices with their start and end apart: 20, of which 9 were waited for; matrix products, arithmetic and copies ran while one was open for 0% of the time, Pallas kernels for 7%

profile of v1, /device:TPU:8, one launch (start us, length us, event | category | flops | bytes accessed | tf_op | source)
XLA Modules:
  0.0 150.1 jit_solution(10540578945220787560)
XLA Ops:
  0.0 4.4 %collective-permute-start = (bf16[256,2048]{1,0:T(8,128)(2,1)}, bf16[256,2048]{1,0:T(8,128)(2,1)}, u32[]{:S(2)}, u32[]{:S(2)}) collective-permute-start(bf16[256,2048]{1,0:T(8,128)(2,1)} %bitcast.33), channel_id=1, source_target_pairs={{0,32},{1,33},{2,34},{3,35},{4,36},{5,37},{6,38},{7,39},{8,40},{9,... | collective-permute-start | bytes 3145736 | tf_op jit(solution)/shard_map/ppermute | solution.py:31
  9.4 6.2 %all-to-all-start = ((bf16[4,32,2048]{2,1,0:T(8,128)(2,1)}), bf16[4,32,2048]{2,1,0:T(8,128)(2,1)}, u32[]{:S(2)}, u32[]{:S(2)}) async-start(bf16[4,32,2048]{2,1,0:T(8,128)(2,1)} %bitcast.6), calls=%async_computation | async-start | bytes 1048576 | tf_op jit(solution)/shard_map/all_to_all | solution.py:63
  15.6 1.9 %collective-permute-start.1 = (bf16[192,2048]{1,0:T(8,128)(2,1)S(1)}, bf16[192,2048]{1,0:T(8,128)(2,1)S(1)}, u32[]{:S(2)}, u32[]{:S(2)}) collective-permute-start(bf16[192,2048]{1,0:T(8,128)(2,1)S(1)} %bitcast.18), channel_id=1, source_target_pairs={{0,1},{1,0},{2,3},{3,2},{4,5},{5,4},{6,7},{7,6},{8,9},{9,8},{10,11... | collective-permute-start | bytes 2359304 | tf_op jit(solution)/shard_map/ppermute | solution.py:31
  17.5 2.4 %collective-permute-start.2 = (bf16[192,2048]{1,0:T(8,128)(2,1)S(1)}, bf16[192,2048]{1,0:T(8,128)(2,1)}, u32[]{:S(2)}, u32[]{:S(2)}) collective-permute-start(bf16[192,2048]{1,0:T(8,128)(2,1)S(1)} %bitcast.23), channel_id=1, source_target_pairs={{0,1},{1,0},{2,3},{3,2},{4,5},{5,4},{6,7},{7,6},{8,9},{9,8},{10,11... | collective-permute-start | bytes 2359304 | tf_op jit(solution)/shard_map/ppermute | solution.py:31
  19.9 1.9 %collective-permute-start.3 = (bf16[192,2048]{1,0:T(8,128)(2,1)}, bf16[192,2048]{1,0:T(8,128)(2,1)}, u32[]{:S(2)}, u32[]{:S(2)}) collective-permute-start(bf16[192,2048]{1,0:T(8,128)(2,1)} %bitcast.28), channel_id=1, source_target_pairs={{0,1},{1,0},{2,3},{3,2},{4,5},{5,4},{6,7},{7,6},{8,9},{9,8},{10,11... | collective-permute-start | bytes 2359304 | tf_op jit(solution)/shard_map/ppermute | solution.py:31
  21.9 8.3 %all-to-all-done = bf16[4,32,2048]{2,1,0:T(8,128)(2,1)} async-done(((bf16[4,32,2048]{2,1,0:T(8,128)(2,1)}), bf16[4,32,2048]{2,1,0:T(8,128)(2,1)}, u32[]{:S(2)}, u32[]{:S(2)}) %all-to-all-start) | async-done | bytes 524320 | tf_op jit(solution)/shard_map/all_to_all | solution.py:63
  30.2 3.5 %collective-permute-done.tokens_ref = bf16[256,2048]{1,0:T(8,128)(2,1)} collective-permute-done((bf16[256,2048]{1,0:T(8,128)(2,1)}, bf16[256,2048]{1,0:T(8,128)(2,1)}, u32[]{:S(2)}, u32[]{:S(2)}) %collective-permute-start) | collective-permute-done | bytes 1048608 | tf_op jit(solution)/shard_map/ppermute | solution.py:31
  34.8 2.4 %collective-permute-start.7 = (bf16[128,2048]{1,0:T(8,128)(2,1)S(1)}, bf16[128,2048]{1,0:T(8,128)(2,1)S(1)}, u32[]{:S(2)}, u32[]{:S(2)}) collective-permute-start(bf16[128,2048]{1,0:T(8,128)(2,1)S(1)} %get-tuple-element.32.refs_2_), channel_id=1, source_target_pairs={{0,4},{1,5},{2,6},{3,7},{4,0},{5,1},{6,2},{7,3},{8,12},{9,13},{10,... | collective-permute-start | bytes 1572872 | tf_op jit(solution)/shard_map/ppermute | solution.py:31
  37.2 8.4 %collective-permute-start.5 = (bf16[64,2048]{1,0:T(8,128)(2,1)S(1)}, bf16[64,2048]{1,0:T(8,128)(2,1)S(1)}, u32[]{:S(2)}, u32[]{:S(2)}) collective-permute-start(bf16[64,2048]{1,0:T(8,128)(2,1)S(1)} %get-tuple-element.31), channel_id=1, source_target_pairs={{0,2},{1,3},{2,0},{3,1},{4,6},{5,7},{6,4},{7,5},{8,10},{9,11},{10,... | collective-permute-start | bytes 786440 | tf_op jit(solution)/shard_map/ppermute | solution.py:31
  45.6 1.9 %collective-permute-start.4 = (bf16[64,2048]{1,0:T(8,128)(2,1)S(1)}, bf16[64,2048]{1,0:T(8,128)(2,1)S(1)}, u32[]{:S(2)}, u32[]{:S(2)}) collective-permute-start(bf16[64,2048]{1,0:T(8,128)(2,1)S(1)} %get-tuple-element.30), channel_id=1, source_target_pairs={{0,2},{1,3},{2,0},{3,1},{4,6},{5,7},{6,4},{7,5},{8,10},{9,11},{10,... | collective-permute-start | bytes 786440 | tf_op jit(solution)/shard_map/ppermute | solution.py:31
  47.5 6.7 %collective-permute-done.5.refs_0_ = bf16[64,2048]{1,0:T(8,128)(2,1)S(1)} collective-permute-done((bf16[64,2048]{1,0:T(8,128)(2,1)S(1)}, bf16[64,2048]{1,0:T(8,128)(2,1)S(1)}, u32[]{:S(2)}, u32[]{:S(2)}) %collective-permute-start.5) | collective-permute-done | bytes 262176 | tf_op jit(solution)/shard_map/ppermute | solution.py:31
  54.2 5.8 %collective-permute-start.6 = (bf16[64,2048]{1,0:T(8,128)(2,1)S(1)}, bf16[64,2048]{1,0:T(8,128)(2,1)S(1)}, u32[]{:S(2)}, u32[]{:S(2)}) collective-permute-start(bf16[64,2048]{1,0:T(8,128)(2,1)S(1)} %collective-permute-done.5.refs_0_), channel_id=1, source_target_pairs={{0,4},{1,5},{2,6},{3,7},{4,0},{5,1},{6,2},{7,3},{8,12},{9,13},{10,... | collective-permute-start | bytes 786440 | tf_op jit(solution)/shard_map/ppermute | solution.py:31
  60.0 2.9 %shard_map.75 = bf16[128,2048]{1,0:T(8,128)(2,1)S(1)} custom-call(bf16[128,2048]{1,0:T(8,128)(2,1)S(1)} %collective-permute-done.7.refs_0_, bf16[192,2048]{1,0:T(8,128)(2,1)S(1)} %bitcast.19, bf16[192,2048]{1,0:T(8,128)(2,1)S(1)} %bitcast.24, bf16[192,2048]{1,0:T(8,128)(2,1)S(1)} %bitcast.29, bf16[192,2048]{1,0:T(8,128)(2,1)S(1)} %collective-permute-done.1.refs_4_.refs_6_, ...), custom_call_target="tpu_custom_call" | custom-call | tf_op jit(solution)/shard_map/pallas_call | solution.py:70
  64.3 2.9 %shard_map.77 = bf16[64,2048]{1,0:T(8,128)(2,1)S(1)} custom-call(bf16[64,2048]{1,0:T(8,128)(2,1)S(1)} %collective-permute-done.6.refs_0_, bf16[192,2048]{1,0:T(8,128)(2,1)S(1)} %bitcast.20, bf16[192,2048]{1,0:T(8,128)(2,1)S(1)} %bitcast.25, bf16[192,2048]{1,0:T(8,128)(2,1)S(1)} %bitcast.30, bf16[192,2048]{1,0:T(8,128)(2,1)S(1)} %collective-permute-done.1.refs_4_.refs_6_, ...), custom_call_target="tpu_custom_call" | custom-call | tf_op jit(solution)/shard_map/pallas_call | solution.py:70
  67.2 3.9 %collective-permute-start.10 = (bf16[64,2048]{1,0:T(8,128)(2,1)S(1)}, bf16[64,2048]{1,0:T(8,128)(2,1)S(1)}, u32[]{:S(2)}, u32[]{:S(2)}) collective-permute-start(bf16[64,2048]{1,0:T(8,128)(2,1)S(1)} %shard_map.77), channel_id=1, source_target_pairs={{0,4},{1,5},{2,6},{3,7},{4,0},{5,1},{6,2},{7,3},{8,12},{9,13},{10,... | collective-permute-start | bytes 786440 | tf_op jit(solution)/shard_map/ppermute | solution.py:31
  71.1 1.9 %collective-permute-start.9 = (bf16[64,2048]{1,0:T(8,128)(2,1)S(1)}, bf16[64,2048]{1,0:T(8,128)(2,1)S(1)}, u32[]{:S(2)}, u32[]{:S(2)}) collective-permute-start(bf16[64,2048]{1,0:T(8,128)(2,1)S(1)} %collective-permute-done.4.refs_1_), channel_id=1, source_target_pairs={{0,4},{1,5},{2,6},{3,7},{4,0},{5,1},{6,2},{7,3},{8,12},{9,13},{10,... | collective-permute-start | bytes 786440 | tf_op jit(solution)/shard_map/ppermute | solution.py:31
  73.0 3.3 %shard_map.76.mine_ref = f32[256,2048]{1,0:T(8,128)S(1)} custom-call(bf16[64,2048]{1,0:T(8,128)(2,1)S(1)} %collective-permute-done.5.refs_0_, bf16[64,2048]{1,0:T(8,128)(2,1)S(1)} %collective-permute-done.4.refs_1_, bf16[128,2048]{1,0:T(8,128)(2,1)S(1)} %get-tuple-element.32.refs_2_, bf16[192,2048]{1,0:T(8,128)(2,1)S(1)} %bitcast.21, ...), custom_call_target="tpu_custom_call" | custom-call | tf_op jit(solution)/shard_map/pallas_call | solution.py:70
  78.3 2.8 %collective-permute-start.11 = (bf16[128,2048]{1,0:T(8,128)(2,1)S(1)}, bf16[128,2048]{1,0:T(8,128)(2,1)S(1)}, u32[]{:S(2)}, u32[]{:S(2)}) collective-permute-start(bf16[128,2048]{1,0:T(8,128)(2,1)S(1)} %shard_map.75), channel_id=1, source_target_pairs={{0,4},{1,5},{2,6},{3,7},{4,0},{5,1},{6,2},{7,3},{8,12},{9,13},{10,... | collective-permute-start | bytes 1572872 | tf_op jit(solution)/shard_map/ppermute | solution.py:31
  81.1 2.8 %collective-permute-done.9.refs_0_ = bf16[64,2048]{1,0:T(8,128)(2,1)S(1)} collective-permute-done((bf16[64,2048]{1,0:T(8,128)(2,1)S(1)}, bf16[64,2048]{1,0:T(8,128)(2,1)S(1)}, u32[]{:S(2)}, u32[]{:S(2)}) %collective-permute-start.9) | collective-permute-done | bytes 262176 | tf_op jit(solution)/shard_map/ppermute | solution.py:31
  83.9 2.9 %shard_map.80 = bf16[64,2048]{1,0:T(8,128)(2,1)S(1)} custom-call(bf16[64,2048]{1,0:T(8,128)(2,1)S(1)} %collective-permute-done.9.refs_0_, bf16[192,2048]{1,0:T(8,128)(2,1)S(1)} %bitcast.22, bf16[192,2048]{1,0:T(8,128)(2,1)S(1)} %bitcast.27, bf16[192,2048]{1,0:T(8,128)(2,1)S(1)} %bitcast.32, bf16[192,2048]{1,0:T(8,128)(2,1)S(1)} %collective-permute-done.1.refs_4_.refs_6_, ...), custom_call_target="tpu_custom_call" | custom-call | tf_op jit(solution)/shard_map/pallas_call | solution.py:70
  86.7 2.6 %collective-permute-start.15 = (bf16[64,2048]{1,0:T(8,128)(2,1)S(1)}, bf16[64,2048]{1,0:T(8,128)(2,1)S(1)}, u32[]{:S(2)}, u32[]{:S(2)}) collective-permute-start(bf16[64,2048]{1,0:T(8,128)(2,1)S(1)} %shard_map.80), channel_id=1, source_target_pairs={{0,4},{1,5},{2,6},{3,7},{4,0},{5,1},{6,2},{7,3},{8,12},{9,13},{10,... | collective-permute-start | bytes 786440 | tf_op jit(solution)/shard_map/ppermute | solution.py:31
  89.4 9.7 %collective-permute-start.12 = (bf16[64,2048]{1,0:T(8,128)(2,1)S(1)}, bf16[64,2048]{1,0:T(8,128)(2,1)S(1)}, u32[]{:S(2)}, u32[]{:S(2)}) collective-permute-start(bf16[64,2048]{1,0:T(8,128)(2,1)S(1)} %shard_map.78), channel_id=1, source_target_pairs={{0,2},{1,3},{2,0},{3,1},{4,6},{5,7},{6,4},{7,5},{8,10},{9,11},{10,... | collective-permute-start | bytes 786440 | tf_op jit(solution)/shard_map/ppermute | solution.py:31
  99.1 6.3 %collective-permute-start.16 = (bf16[64,2048]{1,0:T(8,128)(2,1)S(1)}, bf16[64,2048]{1,0:T(8,128)(2,1)S(1)}, u32[]{:S(2)}, u32[]{:S(2)}) collective-permute-start(bf16[64,2048]{1,0:T(8,128)(2,1)S(1)} %shard_map.81), channel_id=1, source_target_pairs={{0,2},{1,3},{2,0},{3,1},{4,6},{5,7},{6,4},{7,5},{8,10},{9,11},{10,... | collective-permute-start | bytes 786440 | tf_op jit(solution)/shard_map/ppermute | solution.py:31
  105.4 6.3 %collective-permute-start.8 = (f32[128,256]{1,0:T(8,128)S(1)}, f32[128,256]{1,0:T(8,128)S(1)}, u32[]{:S(2)}, u32[]{:S(2)}) collective-permute-start(f32[128,256]{1,0:T(8,128)S(1)} %get-tuple-element.37), channel_id=1, source_target_pairs={{0,32},{1,33},{2,34},{3,35},{4,36},{5,37},{6,38},{7,39},{8,40},{9,... | collective-permute-start | bytes 393224 | tf_op jit(solution)/shard_map/ppermute | solution.py:31
  111.8 10.3 %collective-permute-start.13 = (bf16[32,2048]{1,0:T(8,128)(2,1)S(1)}, bf16[32,2048]{1,0:T(8,128)(2,1)S(1)}, u32[]{:S(2)}, u32[]{:S(2)}) collective-permute-start(bf16[32,2048]{1,0:T(8,128)(2,1)S(1)} %get-tuple-element.44), channel_id=1, source_target_pairs={{0,32},{1,33},{2,34},{3,35},{4,36},{5,37},{6,38},{7,39},{8,40},{9,... | collective-permute-start | bytes 393224 | tf_op jit(solution)/shard_map/ppermute | solution.py:31
  122.1 1.9 %collective-permute-start.14 = (bf16[32,2048]{1,0:T(8,128)(2,1)S(1)}, bf16[32,2048]{1,0:T(8,128)(2,1)S(1)}, u32[]{:S(2)}, u32[]{:S(2)}) collective-permute-start(bf16[32,2048]{1,0:T(8,128)(2,1)S(1)} %get-tuple-element.45), channel_id=1, source_target_pairs={{0,56},{1,57},{2,58},{3,59},{4,60},{5,61},{6,62},{7,63},{8,32},{9,... | collective-permute-start | bytes 393224 | tf_op jit(solution)/shard_map/ppermute | solution.py:31
  124.1 7.2 %collective-permute-start.17 = (bf16[32,2048]{1,0:T(8,128)(2,1)S(1)}, bf16[32,2048]{1,0:T(8,128)(2,1)S(1)}, u32[]{:S(2)}, u32[]{:S(2)}) collective-permute-start(bf16[32,2048]{1,0:T(8,128)(2,1)S(1)} %get-tuple-element.47), channel_id=1, source_target_pairs={{0,48},{1,49},{2,50},{3,51},{4,52},{5,53},{6,54},{7,55},{8,56},{9,... | collective-permute-start | bytes 393224 | tf_op jit(solution)/shard_map/ppermute | solution.py:31
  131.3 1.9 %collective-permute-start.18 = (bf16[32,2048]{1,0:T(8,128)(2,1)S(1)}, bf16[32,2048]{1,0:T(8,128)(2,1)S(1)}, u32[]{:S(2)}, u32[]{:S(2)}) collective-permute-start(bf16[32,2048]{1,0:T(8,128)(2,1)S(1)} %get-tuple-element.48), channel_id=1, source_target_pairs={{0,40},{1,41},{2,42},{3,43},{4,44},{5,45},{6,46},{7,47},{8,48},{9,... | collective-permute-start | bytes 393224 | tf_op jit(solution)/shard_map/ppermute | solution.py:31
  133.2 3.0 %collective-permute-done.14.refs_1_ = bf16[32,2048]{1,0:T(8,128)(2,1)S(1)} collective-permute-done((bf16[32,2048]{1,0:T(8,128)(2,1)S(1)}, bf16[32,2048]{1,0:T(8,128)(2,1)S(1)}, u32[]{:S(2)}, u32[]{:S(2)}) %collective-permute-start.14) | collective-permute-done | bytes 131104 | tf_op jit(solution)/shard_map/ppermute | solution.py:31
  136.2 5.2 %collective-permute-done.17.refs_2_ = bf16[32,2048]{1,0:T(8,128)(2,1)S(1)} collective-permute-done((bf16[32,2048]{1,0:T(8,128)(2,1)S(1)}, bf16[32,2048]{1,0:T(8,128)(2,1)S(1)}, u32[]{:S(2)}, u32[]{:S(2)}) %collective-permute-start.17) | collective-permute-done | bytes 131104 | tf_op jit(solution)/shard_map/ppermute | solution.py:31
  141.4 5.8 %collective-permute-done.18.refs_3_ = bf16[32,2048]{1,0:T(8,128)(2,1)S(1)} collective-permute-done((bf16[32,2048]{1,0:T(8,128)(2,1)S(1)}, bf16[32,2048]{1,0:T(8,128)(2,1)S(1)}, u32[]{:S(2)}, u32[]{:S(2)}) %collective-permute-start.18) | collective-permute-done | bytes 131104 | tf_op jit(solution)/shard_map/ppermute | solution.py:31
  147.2 2.9 %shard_map.83 = bf16[256,2048]{1,0:T(8,128)(2,1)} custom-call(bf16[256,2048]{1,0:T(8,128)(2,1)} %collective-permute-done.tokens_ref, f32[128,256]{1,0:T(8,128)S(1)} %collective-permute-done.8.weight_ref, bf16[32,2048]{1,0:T(8,128)(2,1)S(1)} %collective-permute-done.13.refs_0_, bf16[32,2048]{1,0:T(8,128)(2,1)S(1)} %collective-permute-done.14.refs_1_, ...), custom_call_target="tpu_custom_call" | custom-call | tf_op jit(solution)/shard_map/pallas_call | solution.py:70
  (33 shorter events, 9.6 us)
Async XLA Ops:
  0.0 15.6 %copy-start = (bf16[1,1,2048,192]{2,3,1,0:T(8,128)(2,1)S(1)}, bf16[1,1,2048,192]{2,3,1,0:T(8,128)(2,1)}, u32[]{:S(2)}) copy-start(bf16[1,1,2048,192]{2,3,1,0:T(8,128)(2,1)} %param.9) | copy-start | bytes 2359300
  0.0 17.5 %copy-start.1 = (bf16[1,1,2048,192]{2,3,1,0:T(8,128)(2,1)S(1)}, bf16[1,1,2048,192]{2,3,1,0:T(8,128)(2,1)}, u32[]{:S(2)}) copy-start(bf16[1,1,2048,192]{2,3,1,0:T(8,128)(2,1)} %param.10) | copy-start | bytes 2359300
  0.0 60.0 %copy-start.2 = (bf16[1,1,192,2048]{3,2,1,0:T(8,128)(2,1)S(1)}, bf16[1,1,192,2048]{3,2,1,0:T(8,128)(2,1)}, u32[]{:S(2)}) copy-start(bf16[1,1,192,2048]{3,2,1,0:T(8,128)(2,1)} %param.11) | copy-start | bytes 2359300
  0.0 33.7 %collective-permute-start = (bf16[256,2048]{1,0:T(8,128)(2,1)}, bf16[256,2048]{1,0:T(8,128)(2,1)}, u32[]{:S(2)}, u32[]{:S(2)}) collective-permute-start(bf16[256,2048]{1,0:T(8,128)(2,1)} %bitcast.33), channel_id=1, source_target_pairs={{0,32},{1,33},{2,34},{3,35},{4,36},{5,37},{6,38},{7,39},{8,40},{9,... | collective-permute-start | bytes 3145736 | tf_op jit(solution)/shard_map/ppermute | solution.py:31
  4.4 1.3 copy-start.3
  5.7 0.7 copy-start.4
  6.4 0.7 copy-start.5
  7.1 0.7 copy-start.6
  9.4 20.8 %all-to-all-start = ((bf16[4,32,2048]{2,1,0:T(8,128)(2,1)}), bf16[4,32,2048]{2,1,0:T(8,128)(2,1)}, u32[]{:S(2)}, u32[]{:S(2)}) async-start(bf16[4,32,2048]{2,1,0:T(8,128)(2,1)} %bitcast.6), calls=%async_computation | async-start | bytes 1048576 | tf_op jit(solution)/shard_map/all_to_all | solution.py:63
  15.6 14.6 %collective-permute-start.1 = (bf16[192,2048]{1,0:T(8,128)(2,1)S(1)}, bf16[192,2048]{1,0:T(8,128)(2,1)S(1)}, u32[]{:S(2)}, u32[]{:S(2)}) collective-permute-start(bf16[192,2048]{1,0:T(8,128)(2,1)S(1)} %bitcast.18), channel_id=1, source_target_pairs={{0,1},{1,0},{2,3},{3,2},{4,5},{5,4},{6,7},{7,6},{8,9},{9,8},{10,11... | collective-permute-start | bytes 2359304 | tf_op jit(solution)/shard_map/ppermute | solution.py:31
  17.5 12.7 %collective-permute-start.2 = (bf16[192,2048]{1,0:T(8,128)(2,1)S(1)}, bf16[192,2048]{1,0:T(8,128)(2,1)}, u32[]{:S(2)}, u32[]{:S(2)}) collective-permute-start(bf16[192,2048]{1,0:T(8,128)(2,1)S(1)} %bitcast.23), channel_id=1, source_target_pairs={{0,1},{1,0},{2,3},{3,2},{4,5},{5,4},{6,7},{7,6},{8,9},{9,8},{10,11... | collective-permute-start | bytes 2359304 | tf_op jit(solution)/shard_map/ppermute | solution.py:31
  19.9 10.3 %collective-permute-start.3 = (bf16[192,2048]{1,0:T(8,128)(2,1)}, bf16[192,2048]{1,0:T(8,128)(2,1)}, u32[]{:S(2)}, u32[]{:S(2)}) collective-permute-start(bf16[192,2048]{1,0:T(8,128)(2,1)} %bitcast.28), channel_id=1, source_target_pairs={{0,1},{1,0},{2,3},{3,2},{4,5},{5,4},{6,7},{7,6},{8,9},{9,8},{10,11... | collective-permute-start | bytes 2359304 | tf_op jit(solution)/shard_map/ppermute | solution.py:31
  34.8 25.2 %collective-permute-start.7 = (bf16[128,2048]{1,0:T(8,128)(2,1)S(1)}, bf16[128,2048]{1,0:T(8,128)(2,1)S(1)}, u32[]{:S(2)}, u32[]{:S(2)}) collective-permute-start(bf16[128,2048]{1,0:T(8,128)(2,1)S(1)} %get-tuple-element.32.refs_2_), channel_id=1, source_target_pairs={{0,4},{1,5},{2,6},{3,7},{4,0},{5,1},{6,2},{7,3},{8,12},{9,13},{10,... | collective-permute-start | bytes 1572872 | tf_op jit(solution)/shard_map/ppermute | solution.py:31
  37.2 17.0 %collective-permute-start.5 = (bf16[64,2048]{1,0:T(8,128)(2,1)S(1)}, bf16[64,2048]{1,0:T(8,128)(2,1)S(1)}, u32[]{:S(2)}, u32[]{:S(2)}) collective-permute-start(bf16[64,2048]{1,0:T(8,128)(2,1)S(1)} %get-tuple-element.31), channel_id=1, source_target_pairs={{0,2},{1,3},{2,0},{3,1},{4,6},{5,7},{6,4},{7,5},{8,10},{9,11},{10,... | collective-permute-start | bytes 786440 | tf_op jit(solution)/shard_map/ppermute | solution.py:31
  45.6 17.4 %collective-permute-start.4 = (bf16[64,2048]{1,0:T(8,128)(2,1)S(1)}, bf16[64,2048]{1,0:T(8,128)(2,1)S(1)}, u32[]{:S(2)}, u32[]{:S(2)}) collective-permute-start(bf16[64,2048]{1,0:T(8,128)(2,1)S(1)} %get-tuple-element.30), channel_id=1, source_target_pairs={{0,2},{1,3},{2,0},{3,1},{4,6},{5,7},{6,4},{7,5},{8,10},{9,11},{10,... | collective-permute-start | bytes 786440 | tf_op jit(solution)/shard_map/ppermute | solution.py:31
  54.2 10.1 %collective-permute-start.6 = (bf16[64,2048]{1,0:T(8,128)(2,1)S(1)}, bf16[64,2048]{1,0:T(8,128)(2,1)S(1)}, u32[]{:S(2)}, u32[]{:S(2)}) collective-permute-start(bf16[64,2048]{1,0:T(8,128)(2,1)S(1)} %collective-permute-done.5.refs_0_), channel_id=1, source_target_pairs={{0,4},{1,5},{2,6},{3,7},{4,0},{5,1},{6,2},{7,3},{8,12},{9,13},{10,... | collective-permute-start | bytes 786440 | tf_op jit(solution)/shard_map/ppermute | solution.py:31
  67.2 11.1 %collective-permute-start.10 = (bf16[64,2048]{1,0:T(8,128)(2,1)S(1)}, bf16[64,2048]{1,0:T(8,128)(2,1)S(1)}, u32[]{:S(2)}, u32[]{:S(2)}) collective-permute-start(bf16[64,2048]{1,0:T(8,128)(2,1)S(1)} %shard_map.77), channel_id=1, source_target_pairs={{0,4},{1,5},{2,6},{3,7},{4,0},{5,1},{6,2},{7,3},{8,12},{9,13},{10,... | collective-permute-start | bytes 786440 | tf_op jit(solution)/shard_map/ppermute | solution.py:31
  71.1 12.8 %collective-permute-start.9 = (bf16[64,2048]{1,0:T(8,128)(2,1)S(1)}, bf16[64,2048]{1,0:T(8,128)(2,1)S(1)}, u32[]{:S(2)}, u32[]{:S(2)}) collective-permute-start(bf16[64,2048]{1,0:T(8,128)(2,1)S(1)} %collective-permute-done.4.refs_1_), channel_id=1, source_target_pairs={{0,4},{1,5},{2,6},{3,7},{4,0},{5,1},{6,2},{7,3},{8,12},{9,13},{10,... | collective-permute-start | bytes 786440 | tf_op jit(solution)/shard_map/ppermute | solution.py:31
  78.3 33.5 %collective-permute-start.11 = (bf16[128,2048]{1,0:T(8,128)(2,1)S(1)}, bf16[128,2048]{1,0:T(8,128)(2,1)S(1)}, u32[]{:S(2)}, u32[]{:S(2)}) collective-permute-start(bf16[128,2048]{1,0:T(8,128)(2,1)S(1)} %shard_map.75), channel_id=1, source_target_pairs={{0,4},{1,5},{2,6},{3,7},{4,0},{5,1},{6,2},{7,3},{8,12},{9,13},{10,... | collective-permute-start | bytes 1572872 | tf_op jit(solution)/shard_map/ppermute | solution.py:31
  86.7 12.3 %collective-permute-start.15 = (bf16[64,2048]{1,0:T(8,128)(2,1)S(1)}, bf16[64,2048]{1,0:T(8,128)(2,1)S(1)}, u32[]{:S(2)}, u32[]{:S(2)}) collective-permute-start(bf16[64,2048]{1,0:T(8,128)(2,1)S(1)} %shard_map.80), channel_id=1, source_target_pairs={{0,4},{1,5},{2,6},{3,7},{4,0},{5,1},{6,2},{7,3},{8,12},{9,13},{10,... | collective-permute-start | bytes 786440 | tf_op jit(solution)/shard_map/ppermute | solution.py:31
  89.4 22.3 %collective-permute-start.12 = (bf16[64,2048]{1,0:T(8,128)(2,1)S(1)}, bf16[64,2048]{1,0:T(8,128)(2,1)S(1)}, u32[]{:S(2)}, u32[]{:S(2)}) collective-permute-start(bf16[64,2048]{1,0:T(8,128)(2,1)S(1)} %shard_map.78), channel_id=1, source_target_pairs={{0,2},{1,3},{2,0},{3,1},{4,6},{5,7},{6,4},{7,5},{8,10},{9,11},{10,... | collective-permute-start | bytes 786440 | tf_op jit(solution)/shard_map/ppermute | solution.py:31
  99.1 24.9 %collective-permute-start.16 = (bf16[64,2048]{1,0:T(8,128)(2,1)S(1)}, bf16[64,2048]{1,0:T(8,128)(2,1)S(1)}, u32[]{:S(2)}, u32[]{:S(2)}) collective-permute-start(bf16[64,2048]{1,0:T(8,128)(2,1)S(1)} %shard_map.81), channel_id=1, source_target_pairs={{0,2},{1,3},{2,0},{3,1},{4,6},{5,7},{6,4},{7,5},{8,10},{9,11},{10,... | collective-permute-start | bytes 786440 | tf_op jit(solution)/shard_map/ppermute | solution.py:31
  105.4 27.8 %collective-permute-start.8 = (f32[128,256]{1,0:T(8,128)S(1)}, f32[128,256]{1,0:T(8,128)S(1)}, u32[]{:S(2)}, u32[]{:S(2)}) collective-permute-start(f32[128,256]{1,0:T(8,128)S(1)} %get-tuple-element.37), channel_id=1, source_target_pairs={{0,32},{1,33},{2,34},{3,35},{4,36},{5,37},{6,38},{7,39},{8,40},{9,... | collective-permute-start | bytes 393224 | tf_op jit(solution)/shard_map/ppermute | solution.py:31
  111.8 21.4 %collective-permute-start.13 = (bf16[32,2048]{1,0:T(8,128)(2,1)S(1)}, bf16[32,2048]{1,0:T(8,128)(2,1)S(1)}, u32[]{:S(2)}, u32[]{:S(2)}) collective-permute-start(bf16[32,2048]{1,0:T(8,128)(2,1)S(1)} %get-tuple-element.44), channel_id=1, source_target_pairs={{0,32},{1,33},{2,34},{3,35},{4,36},{5,37},{6,38},{7,39},{8,40},{9,... | collective-permute-start | bytes 393224 | tf_op jit(solution)/shard_map/ppermute | solution.py:31
  122.1 14.1 %collective-permute-start.14 = (bf16[32,2048]{1,0:T(8,128)(2,1)S(1)}, bf16[32,2048]{1,0:T(8,128)(2,1)S(1)}, u32[]{:S(2)}, u32[]{:S(2)}) collective-permute-start(bf16[32,2048]{1,0:T(8,128)(2,1)S(1)} %get-tuple-element.45), channel_id=1, source_target_pairs={{0,56},{1,57},{2,58},{3,59},{4,60},{5,61},{6,62},{7,63},{8,32},{9,... | collective-permute-start | bytes 393224 | tf_op jit(solution)/shard_map/ppermute | solution.py:31
  124.1 17.3 %collective-permute-start.17 = (bf16[32,2048]{1,0:T(8,128)(2,1)S(1)}, bf16[32,2048]{1,0:T(8,128)(2,1)S(1)}, u32[]{:S(2)}, u32[]{:S(2)}) collective-permute-start(bf16[32,2048]{1,0:T(8,128)(2,1)S(1)} %get-tuple-element.47), channel_id=1, source_target_pairs={{0,48},{1,49},{2,50},{3,51},{4,52},{5,53},{6,54},{7,55},{8,56},{9,... | collective-permute-start | bytes 393224 | tf_op jit(solution)/shard_map/ppermute | solution.py:31
  131.3 15.9 %collective-permute-start.18 = (bf16[32,2048]{1,0:T(8,128)(2,1)S(1)}, bf16[32,2048]{1,0:T(8,128)(2,1)S(1)}, u32[]{:S(2)}, u32[]{:S(2)}) collective-permute-start(bf16[32,2048]{1,0:T(8,128)(2,1)S(1)} %get-tuple-element.48), channel_id=1, source_target_pairs={{0,40},{1,41},{2,42},{3,43},{4,44},{5,45},{6,46},{7,47},{8,48},{9,... | collective-permute-start | bytes 393224 | tf_op jit(solution)/shard_map/ppermute | solution.py:31

commit v2 on v1

v2 whole, which is shorter than its diff:
```python
import functools

import jax
import jax.numpy as jnp
from jax import lax
from jax.experimental import pallas as pl
from jax.experimental.pallas import tpu as pltpu
from jax.sharding import PartitionSpec as P

CAP = 32
WAVE = 4
EPSILON = 1e-06
N_Y, N_Z, N_CORE = 8, 2, 2
BF16, F32 = jnp.bfloat16, jnp.float32
ROOM = 24 * 1024 * 1024
ORDER = (0, 1, 3, 2)
VMEM = pl.BlockSpec(memory_space=pltpu.VMEM)


def permuted(x, move, sections=1, by=0):
    pairs = []
    for sec in range(sections):
        for y in range(N_Y):
            for z in range(N_Z):
                for core in range(N_CORE):
                    y2, z2, core2 = move(y, z, core)
                    source = (y * N_Z + z) * N_CORE + core
                    target = ((y2 % N_Y) * N_Z + z2) * N_CORE + core2
                    lanes = N_Y * N_Z * N_CORE
                    pairs.append((sec * lanes + source, ((sec + by) % sections) * lanes + target))
    return lax.ppermute(x, "ep" if sections == 1 else ("pp", "ep"), pairs)


def other_core(x):
    return permuted(x, lambda y, z, core: (y, z, 1 - core))


def other_plane(x):
    return permuted(x, lambda y, z, core: (y, 1 - z, core))


def pair_swap(x):
    return permuted(x, lambda y, z, core: (y ^ 1, z, core))


def stay(y, z, core):
    return y, z, core


def exchanged(x, planes):
    groups = []
    for parity in range(2):
        for core in range(N_CORE):
            members = [
                [((2 * half + parity) * N_Z + z) * N_CORE + core for z in range(N_Z)]
                for half in range(WAVE)
            ]
            if planes == N_Z:
                groups.append(sum(members, []))
            else:
                groups += [[member[z] for member in members] for z in range(N_Z)]
    parts = x.reshape(len(groups[0]), -1, x.shape[-1])
    parts = lax.all_to_all(
        parts, "ep", split_axis=0, concat_axis=0, axis_index_groups=groups, tiled=True
    )
    return parts.reshape(x.shape)


def called(kernel, out_shape, *xs, scalars=0):
    return pl.pallas_call(
        kernel,
        out_shape=out_shape,
        in_specs=[pl.BlockSpec(memory_space=pltpu.SMEM)] * scalars + [VMEM] * (len(xs) - scalars),
        out_specs=jax.tree.map(lambda _: VMEM, out_shape),
        compiler_params=pltpu.CompilerParams(vmem_limit_bytes=ROOM),
        cost_estimate=pl.CostEstimate(flops=0, bytes_accessed=0, transcendentals=0),
    )(*xs)


def pack_kernel(place_ref, tokens_ref, gain_ref, routes_ref, mixing_ref, packed_ref, weight_ref):
    widened = tokens_ref[...].astype(F32)
    scale = lax.rsqrt(jnp.mean(widened * widened, axis=-1, keepdims=True) + EPSILON)
    normed = (widened * scale * gain_ref[...].astype(F32)).astype(BF16)
    rows = tokens_ref.shape[0]
    shape = (WAVE * CAP, rows)
    row = lax.broadcasted_iota(jnp.int32, shape, 0)
    member = jnp.zeros(shape, F32)
    weight = jnp.zeros(shape, F32)
    for k in range(routes_ref.shape[0]):
        hit = routes_ref[k : k + 1, :] == row // CAP
        member = jnp.where(hit, 1.0, member)
        weight = weight + jnp.where(hit, mixing_ref[k : k + 1, :], 0.0)
    upto = lax.broadcasted_iota(jnp.int32, (rows, rows), 0) <= lax.broadcasted_iota(
        jnp.int32, (rows, rows), 1
    )
    count = jnp.dot(
        member.astype(BF16), jnp.where(upto, 1.0, 0.0).astype(BF16), preferred_element_type=F32
    )
    slot = (row % CAP + 1).astype(F32)
    onehot = jnp.where((count == slot) & (member > 0.0), 1.0, 0.0)
    weight = weight * onehot
    for at in range(WAVE):
        start = (at + WAVE - place_ref[0]) % WAVE * CAP
        weight_ref[pl.ds(pl.multiple_of(start, CAP), CAP)] = weight[at * CAP : (at + 1) * CAP]
    packed = jnp.dot(onehot.astype(BF16), normed, preferred_element_type=F32).astype(BF16)
    for at in range(N_Z * WAVE):
        chunk = at // N_Z * CAP
        packed_ref[at * CAP : (at + 1) * CAP] = packed[chunk : chunk + CAP]


def stack_kernel(*refs):
    count = len(refs) // 3
    for index, out in enumerate(refs[2 * count :]):
        rows = refs[2 * index].shape[0]
        out[:rows] = refs[2 * index][...]
        out[rows:] = refs[2 * index + 1][...]


def sort_kernel(place_ref, held_ref, far_ref, near_ref):
    for other, out_ref in ((1, far_ref), (0, near_ref)):
        plane = (place_ref[1] + other) % N_Z
        for index, k in enumerate(ORDER):
            at = ((place_ref[0] + WAVE - k) % WAVE * N_Z + plane) * CAP
            out_ref[index * CAP : (index + 1) * CAP] = held_ref[pl.ds(pl.multiple_of(at, CAP), CAP)]


def hidden_rows(rows, gates, ups):
    across = (((1,), (1,)), ((), ()))
    gate_proj = lax.dot_general(rows, gates[...], across, preferred_element_type=F32)
    up_proj = lax.dot_general(rows, ups[...], across, preferred_element_type=F32)
    return (jax.nn.silu(gate_proj) * up_proj).astype(BF16)


def hidden_kernel(rows_ref, gates, ups, out_ref):
    out_ref[...] = hidden_rows(rows_ref[...], gates, ups)


def mine_kernel(far_ref, near_ref, gates, ups, downs, out_ref):
    rows = jnp.concatenate([far_ref[...], near_ref[...]], axis=0)
    hidden = hidden_rows(rows, gates, ups)
    out_ref[...] = jnp.dot(hidden, downs[...], preferred_element_type=F32)


def sum_kernel(at, hidden_at, mine_ref, hidden_ref, downs, *refs):
    adds, outs = (refs[:1], refs[1:]) if len(refs) == 3 else ((), refs)
    size = sum(out.shape[0] for out in outs)
    total = mine_ref[at : at + size] + jnp.dot(
        hidden_ref[hidden_at : hidden_at + size], downs[...], preferred_element_type=F32
    )
    for add in adds:
        total = total + add[...].astype(F32)
    start = 0
    for out in outs:
        out[...] = total[start : start + out.shape[0]].astype(BF16)
        start += out.shape[0]


def summed(at, hidden_at, size, mine, hidden, downs, *far):
    out = [jax.ShapeDtypeStruct((size, mine.shape[1]), BF16)] * 2
    kernel = functools.partial(sum_kernel, at, hidden_at)
    return called(kernel, out, mine, hidden, downs, *far)


def combine_kernel(tokens_ref, weight_ref, *refs):
    pieces, out_ref = refs[:-1], refs[-1]
    weight = weight_ref[...].T
    high = weight.astype(BF16)
    rest = weight - high.astype(F32)
    middle = rest.astype(BF16)
    low = (rest - middle.astype(F32)).astype(BF16)
    rows = jnp.concatenate([piece[...] for piece in pieces], axis=0)
    total = jnp.dot(
        jnp.concatenate([high, middle], axis=1),
        jnp.concatenate([rows, rows], axis=0),
        preferred_element_type=F32,
    )
    total = total + jnp.dot(low, rows, preferred_element_type=F32)
    out_ref[...] = (tokens_ref[...].astype(F32) + total).astype(BF16)


def tied(*xs):
    return lax.optimization_barrier(xs)


def body(sections, tokens, gain, gate, up, down, routes, mixing):
    tokens, gate, up, down = tokens[0], gate[0, 0].T, up[0, 0].T, down[0, 0]
    rows, features = tokens.shape
    slots, half = WAVE * CAP, 2 * CAP
    ep = lax.axis_index("ep").astype(jnp.int32)
    place = jnp.stack([ep // (2 * N_Z * N_CORE), ep // N_CORE % N_Z])

    packed, weight = called(
        pack_kernel,
        [
            jax.ShapeDtypeStruct((N_Z * slots, features), BF16),
            jax.ShapeDtypeStruct((slots, rows), F32),
        ],
        place,
        tokens,
        gain,
        routes[0].T,
        mixing[0].T,
        scalars=1,
    )

    pairs = ((gate, other_core(gate)), (up, other_core(up)), (down, other_core(down)))
    stack = jax.ShapeDtypeStruct((2 * up.shape[0], features), BF16)
    held, weight, gates, ups, downs = tied(
        exchanged(packed, N_Z),
        permuted(weight, stay, sections, 1),
        *called(stack_kernel, [stack] * 3, *[mat for both in pairs for mat in both]),
    )
    twin_down = pair_swap(down)

    half_rows = jax.ShapeDtypeStruct((slots, features), BF16)
    far, near = called(sort_kernel, [half_rows, half_rows], place, held, scalars=1)
    far, near, tokens = tied(far, near, tokens)
    before = permuted(tokens, stay, sections, 1)
    sums = jax.ShapeDtypeStruct((N_Z * slots, features), F32)
    mine = called(mine_kernel, sums, far, near, gates, ups, downs)
    mine, twin_far, twin_down = tied(mine, pair_swap(far), twin_down)
    (twin_downs,) = called(stack_kernel, [stack], twin_down, other_core(twin_down))
    units = jax.ShapeDtypeStruct((slots, stack.shape[0]), BF16)
    hidden_far = pair_swap(called(hidden_kernel, units, twin_far, gates, ups))
    hidden_far, near, before, twin_downs = tied(hidden_far, near, before, twin_downs)
    hidden_near = pair_swap(called(hidden_kernel, units, pair_swap(near), gates, ups))

    crossing = summed(0, 0, half, mine, hidden_far, twin_downs)
    pieces = []
    for index, part in enumerate(crossing):
        at = index * half
        pieces += summed(
            slots + at, at, CAP, mine, hidden_near, twin_downs, other_plane(part)
        )
    back = {
        k: permuted(piece, lambda y, z, core, k=k: (y - 2 * k, z, core), sections, 1)
        for k, piece in zip(ORDER, pieces)
    }
    return called(
        combine_kernel,
        jax.ShapeDtypeStruct((rows, features), BF16),
        before,
        weight,
        *[back[k] for k in range(WAVE)],
    )[None]


def solution(mesh):
    placed = (
        P("pp", "ep", None),
        P("pp", None),
        P("pp", "ep", None, None),
        P("pp", "ep", None, None),
        P("pp", "ep", None, None),
        P("pp", "ep", None),
        P("pp", "ep", None),
    )
    return jax.shard_map(
        functools.partial(body, mesh.shape["pp"]),
        mesh=mesh,
        in_specs=placed,
        out_specs=P("pp", "ep", None),
        check_vma=False,
    )
```

time: 151 us -> 145 us (0.960)
  the two profiles are of different devices: /device:TPU:8 before, /device:TPU:16 now
where the time goes in v2:
time: 145 us; the launch traced here: 144 us
  starting transfers between devices  65 us (45%)
  waiting for transfers between devices  57.3 us (40%)
  Pallas kernels  13.2 us (9%)
  local copies, waits for them, and re-layouts  8.16 us (6%)
    ppermute x17, waiting for transfers between devices, permuted(): return lax.ppermute(x, 'ep' if sections == 1 else ('pp', 'ep'), pairs)  56.6 us
    ppermute x17, starting transfers between devices, permuted(): return lax.ppermute(x, 'ep' if sections == 1 else ('pp', 'ep'), pairs)  49.2 us
    all_to_all x1, starting transfers between devices, exchanged(): lax.all_to_all(parts, 'ep', split_axis=0, concat_axis=0, axis_index_group...  15.9 us
    pallas_call x11, Pallas kernels, called(): pl.pallas_call(kernel, out_shape=out_shape, in_specs=[pl.BlockSpec(memory...  13.2 us
    unnamed x20, local copies, waits for them, and re-layouts  8.16 us
  transfers between devices with their start and end apart: 18, of which 13 were waited for; matrix products, arithmetic and copies ran while one was open for 0% of the time, Pallas kernels for 6%

profile of v2, /device:TPU:16, one launch (start us, length us, event | category | flops | bytes accessed | tf_op | source)
XLA Modules:
  0.0 144.1 jit_solution(9769214297381923626)
XLA Ops:
  3.4 2.3 %shard_map.73 = (bf16[256,2048]{1,0:T(8,128)(2,1)}, f32[128,256]{1,0:T(8,128)S(1)}) custom-call(s32[2]{0:T(128)S(1)} %pad_add_fusion.place_ref, bf16[256,2048]{1,0:T(8,128)(2,1)S(1)} %bitcast.20, bf16[1,2048]{1,0:T(2,128)(2,1)S(1)} %copy-done.7, s32[8,256]{1,0:T(8,128)S(1)} %bitcast.25, f32[8,256]{1,0:T(8,128)S(1)} %bitcast.26), custom_call_target="tpu_custom_call" | custom-call | tf_op jit(solution)/shard_map/pallas_call | solution.py:70
  5.7 15.9 %all-to-all-start = ((bf16[8,32,2048]{2,1,0:T(8,128)(2,1)}), bf16[8,32,2048]{2,1,0:T(8,128)(2,1)}, u32[]{:S(2)}, u32[]{:S(2)}) async-start(bf16[8,32,2048]{2,1,0:T(8,128)(2,1)} %bitcast.7), calls=%async_computation | async-start | bytes 2097152 | tf_op jit(solution)/shard_map/all_to_all | solution.py:63
  21.6 1.9 %collective-permute-start.1 = (bf16[192,2048]{1,0:T(8,128)(2,1)S(1)}, bf16[192,2048]{1,0:T(8,128)(2,1)S(1)}, u32[]{:S(2)}, u32[]{:S(2)}) collective-permute-start(bf16[192,2048]{1,0:T(8,128)(2,1)S(1)} %bitcast.21), channel_id=1, source_target_pairs={{0,1},{1,0},{2,3},{3,2},{4,5},{5,4},{6,7},{7,6},{8,9},{9,8},{10,11... | collective-permute-start | bytes 2359304 | tf_op jit(solution)/shard_map/ppermute | solution.py:31
  23.5 2.4 %collective-permute-start.2 = (bf16[192,2048]{1,0:T(8,128)(2,1)S(1)}, bf16[192,2048]{1,0:T(8,128)(2,1)S(1)}, u32[]{:S(2)}, u32[]{:S(2)}) collective-permute-start(bf16[192,2048]{1,0:T(8,128)(2,1)S(1)} %bitcast.23), channel_id=1, source_target_pairs={{0,1},{1,0},{2,3},{3,2},{4,5},{5,4},{6,7},{7,6},{8,9},{9,8},{10,11... | collective-permute-start | bytes 2359304 | tf_op jit(solution)/shard_map/ppermute | solution.py:31
  25.9 1.9 %collective-permute-start.3 = (bf16[192,2048]{1,0:T(8,128)(2,1)}, bf16[192,2048]{1,0:T(8,128)(2,1)S(1)}, u32[]{:S(2)}, u32[]{:S(2)}) collective-permute-start(bf16[192,2048]{1,0:T(8,128)(2,1)} %bitcast.15.refs_4_), channel_id=1, source_target_pairs={{0,1},{1,0},{2,3},{3,2},{4,5},{5,4},{6,7},{7,6},{8,9},{9,8},{10,11... | collective-permute-start | bytes 2359304 | tf_op jit(solution)/shard_map/ppermute | solution.py:31
  27.8 2.6 %collective-permute-start.5 = (bf16[192,2048]{1,0:T(8,128)(2,1)}, bf16[192,2048]{1,0:T(8,128)(2,1)}, u32[]{:S(2)}, u32[]{:S(2)}) collective-permute-start(bf16[192,2048]{1,0:T(8,128)(2,1)} %bitcast.15.refs_4_), channel_id=1, source_target_pairs={{0,4},{1,5},{2,6},{3,7},{4,0},{5,1},{6,2},{7,3},{8,12},{9,13},{10,... | collective-permute-start | bytes 2359304 | tf_op jit(solution)/shard_map/ppermute | solution.py:31
  30.4 3.4 %collective-permute-start = (f32[128,256]{1,0:T(8,128)S(1)}, f32[128,256]{1,0:T(8,128)S(1)}, u32[]{:S(2)}, u32[]{:S(2)}) collective-permute-start(f32[128,256]{1,0:T(8,128)S(1)} %get-tuple-element.34), channel_id=1, source_target_pairs={{0,32},{1,33},{2,34},{3,35},{4,36},{5,37},{6,38},{7,39},{8,40},{9,... | collective-permute-start | bytes 393224 | tf_op jit(solution)/shard_map/ppermute | solution.py:31
  36.1 1.4 shard_map.74
  38.8 11.7 %collective-permute-done.weight_ref = f32[128,256]{1,0:T(8,128)S(1)} collective-permute-done((f32[128,256]{1,0:T(8,128)S(1)}, f32[128,256]{1,0:T(8,128)S(1)}, u32[]{:S(2)}, u32[]{:S(2)}) %collective-permute-start) | collective-permute-done | bytes 131104 | tf_op jit(solution)/shard_map/ppermute | solution.py:31
  52.4 5.6 %collective-permute-start.4 = (bf16[128,2048]{1,0:T(8,128)(2,1)S(1)}, bf16[128,2048]{1,0:T(8,128)(2,1)S(1)}, u32[]{:S(2)}, u32[]{:S(2)}) collective-permute-start(bf16[128,2048]{1,0:T(8,128)(2,1)S(1)} %get-tuple-element.41.far_ref), channel_id=1, source_target_pairs={{0,4},{1,5},{2,6},{3,7},{4,0},{5,1},{6,2},{7,3},{8,12},{9,13},{10,... | collective-permute-start | bytes 1572872 | tf_op jit(solution)/shard_map/ppermute | solution.py:31
  58.0 1.9 %collective-permute-start.7 = (bf16[256,2048]{1,0:T(8,128)(2,1)}, bf16[256,2048]{1,0:T(8,128)(2,1)S(1)}, u32[]{:S(2)}, u32[]{:S(2)}) collective-permute-start(bf16[256,2048]{1,0:T(8,128)(2,1)} %bitcast.19), channel_id=1, source_target_pairs={{0,32},{1,33},{2,34},{3,35},{4,36},{5,37},{6,38},{7,39},{8,40},{9,... | collective-permute-start | bytes 3145736 | tf_op jit(solution)/shard_map/ppermute | solution.py:31
  60.0 1.4 copy-done.1
  61.4 1.9 %shard_map.76.mine_ref = f32[256,2048]{1,0:T(8,128)S(1)} custom-call(bf16[128,2048]{1,0:T(8,128)(2,1)S(1)} %get-tuple-element.41.far_ref, bf16[128,2048]{1,0:T(8,128)(2,1)S(1)} %get-tuple-element.52.near_ref, bf16[384,2048]{1,0:T(8,128)(2,1)S(1)} %get-tuple-element.43.gates, bf16[384,2048]{1,0:T(8,128)(2,1)S(1)} %get-tuple-element.44.ups, ...), custom_call_target="tpu_custom_call" | custom-call | tf_op jit(solution)/shard_map/pallas_call | solution.py:70
  63.5 9.7 %collective-permute-done.4.rows_ref = bf16[128,2048]{1,0:T(8,128)(2,1)S(1)} collective-permute-done((bf16[128,2048]{1,0:T(8,128)(2,1)S(1)}, bf16[128,2048]{1,0:T(8,128)(2,1)S(1)}, u32[]{:S(2)}, u32[]{:S(2)}) %collective-permute-start.4) | collective-permute-done | bytes 524320 | tf_op jit(solution)/shard_map/ppermute | solution.py:31
  73.2 1.9 %collective-permute-start.8 = (bf16[192,2048]{1,0:T(8,128)(2,1)}, bf16[192,2048]{1,0:T(8,128)(2,1)S(1)}, u32[]{:S(2)}, u32[]{:S(2)}) collective-permute-start(bf16[192,2048]{1,0:T(8,128)(2,1)} %collective-permute-done.5.refs_0_), channel_id=1, source_target_pairs={{0,1},{1,0},{2,3},{3,2},{4,5},{5,4},{6,7},{7,6},{8,9},{9,8},{10,11... | collective-permute-start | bytes 2359304 | tf_op jit(solution)/shard_map/ppermute | solution.py:31
  76.2 2.4 %collective-permute-start.6 = (bf16[128,384]{1,0:T(8,128)(2,1)S(1)}, bf16[128,384]{1,0:T(8,128)(2,1)S(1)}, u32[]{:S(2)}, u32[]{:S(2)}) collective-permute-start(bf16[128,384]{1,0:T(8,128)(2,1)S(1)} %shard_map.77), channel_id=1, source_target_pairs={{0,4},{1,5},{2,6},{3,7},{4,0},{5,1},{6,2},{7,3},{8,12},{9,13},{10,... | collective-permute-start | bytes 294920 | tf_op jit(solution)/shard_map/ppermute | solution.py:31
  79.8 3.5 %collective-permute-done.6.hidden_ref = bf16[128,384]{1,0:T(8,128)(2,1)S(1)} collective-permute-done((bf16[128,384]{1,0:T(8,128)(2,1)S(1)}, bf16[128,384]{1,0:T(8,128)(2,1)S(1)}, u32[]{:S(2)}, u32[]{:S(2)}) %collective-permute-start.6) | collective-permute-done | bytes 98336 | tf_op jit(solution)/shard_map/ppermute | solution.py:31
  83.3 4.5 %collective-permute-done.7.tokens_ref = bf16[256,2048]{1,0:T(8,128)(2,1)S(1)} collective-permute-done((bf16[256,2048]{1,0:T(8,128)(2,1)}, bf16[256,2048]{1,0:T(8,128)(2,1)S(1)}, u32[]{:S(2)}, u32[]{:S(2)}) %collective-permute-start.7) | collective-permute-done | bytes 1048608 | tf_op jit(solution)/shard_map/ppermute | solution.py:31
  87.8 2.2 %collective-permute-start.9 = (bf16[128,2048]{1,0:T(8,128)(2,1)S(1)}, bf16[128,2048]{1,0:T(8,128)(2,1)S(1)}, u32[]{:S(2)}, u32[]{:S(2)}) collective-permute-start(bf16[128,2048]{1,0:T(8,128)(2,1)S(1)} %get-tuple-element.52.near_ref), channel_id=1, source_target_pairs={{0,4},{1,5},{2,6},{3,7},{4,0},{5,1},{6,2},{7,3},{8,12},{9,13},{10,... | collective-permute-start | bytes 1572872 | tf_op jit(solution)/shard_map/ppermute | solution.py:31
  90.4 8.0 %collective-permute-start.14 = (bf16[64,2048]{1,0:T(8,128)(2,1)S(1)}, bf16[64,2048]{1,0:T(8,128)(2,1)S(1)}, u32[]{:S(2)}, u32[]{:S(2)}) collective-permute-start(bf16[64,2048]{1,0:T(8,128)(2,1)S(1)} %get-tuple-element.58), channel_id=1, source_target_pairs={{0,2},{1,3},{2,0},{3,1},{4,6},{5,7},{6,4},{7,5},{8,10},{9,11},{10,... | collective-permute-start | bytes 786440 | tf_op jit(solution)/shard_map/ppermute | solution.py:31
  98.5 1.9 %collective-permute-start.11 = (bf16[64,2048]{1,0:T(8,128)(2,1)S(1)}, bf16[64,2048]{1,0:T(8,128)(2,1)S(1)}, u32[]{:S(2)}, u32[]{:S(2)}) collective-permute-start(bf16[64,2048]{1,0:T(8,128)(2,1)S(1)} %get-tuple-element.55), channel_id=1, source_target_pairs={{0,2},{1,3},{2,0},{3,1},{4,6},{5,7},{6,4},{7,5},{8,10},{9,11},{10,... | collective-permute-start | bytes 786440 | tf_op jit(solution)/shard_map/ppermute | solution.py:31
  102.3 2.8 %collective-permute-start.10 = (bf16[128,384]{1,0:T(8,128)(2,1)S(1)}, bf16[128,384]{1,0:T(8,128)(2,1)S(1)}, u32[]{:S(2)}, u32[]{:S(2)}) collective-permute-start(bf16[128,384]{1,0:T(8,128)(2,1)S(1)} %shard_map.79), channel_id=1, source_target_pairs={{0,4},{1,5},{2,6},{3,7},{4,0},{5,1},{6,2},{7,3},{8,12},{9,13},{10,... | collective-permute-start | bytes 294920 | tf_op jit(solution)/shard_map/ppermute | solution.py:31
  105.2 11.0 %collective-permute-done.14.refs_0_ = bf16[64,2048]{1,0:T(8,128)(2,1)S(1)} collective-permute-done((bf16[64,2048]{1,0:T(8,128)(2,1)S(1)}, bf16[64,2048]{1,0:T(8,128)(2,1)S(1)}, u32[]{:S(2)}, u32[]{:S(2)}) %collective-permute-start.14) | collective-permute-done | bytes 262176 | tf_op jit(solution)/shard_map/ppermute | solution.py:31
  116.5 1.9 %collective-permute-start.15 = (bf16[32,2048]{1,0:T(8,128)(2,1)S(1)}, bf16[32,2048]{1,0:T(8,128)(2,1)S(1)}, u32[]{:S(2)}, u32[]{:S(2)}) collective-permute-start(bf16[32,2048]{1,0:T(8,128)(2,1)S(1)} %get-tuple-element.59), channel_id=1, source_target_pairs={{0,48},{1,49},{2,50},{3,51},{4,52},{5,53},{6,54},{7,55},{8,56},{9,... | collective-permute-start | bytes 393224 | tf_op jit(solution)/shard_map/ppermute | solution.py:31
  118.5 1.9 %collective-permute-start.16 = (bf16[32,2048]{1,0:T(8,128)(2,1)S(1)}, bf16[32,2048]{1,0:T(8,128)(2,1)S(1)}, u32[]{:S(2)}, u32[]{:S(2)}) collective-permute-start(bf16[32,2048]{1,0:T(8,128)(2,1)S(1)} %get-tuple-element.60), channel_id=1, source_target_pairs={{0,40},{1,41},{2,42},{3,43},{4,44},{5,45},{6,46},{7,47},{8,48},{9,... | collective-permute-start | bytes 393224 | tf_op jit(solution)/shard_map/ppermute | solution.py:31
  120.4 3.2 %collective-permute-done.11.refs_0_ = bf16[64,2048]{1,0:T(8,128)(2,1)S(1)} collective-permute-done((bf16[64,2048]{1,0:T(8,128)(2,1)S(1)}, bf16[64,2048]{1,0:T(8,128)(2,1)S(1)}, u32[]{:S(2)}, u32[]{:S(2)}) %collective-permute-start.11) | collective-permute-done | bytes 262176 | tf_op jit(solution)/shard_map/ppermute | solution.py:31
  124.0 1.9 %collective-permute-start.12 = (bf16[32,2048]{1,0:T(8,128)(2,1)S(1)}, bf16[32,2048]{1,0:T(8,128)(2,1)S(1)}, u32[]{:S(2)}, u32[]{:S(2)}) collective-permute-start(bf16[32,2048]{1,0:T(8,128)(2,1)S(1)} %get-tuple-element.56), channel_id=1, source_target_pairs={{0,32},{1,33},{2,34},{3,35},{4,36},{5,37},{6,38},{7,39},{8,40},{9,... | collective-permute-start | bytes 393224 | tf_op jit(solution)/shard_map/ppermute | solution.py:31
  126.0 4.4 %collective-permute-start.13 = (bf16[32,2048]{1,0:T(8,128)(2,1)S(1)}, bf16[32,2048]{1,0:T(8,128)(2,1)S(1)}, u32[]{:S(2)}, u32[]{:S(2)}) collective-permute-start(bf16[32,2048]{1,0:T(8,128)(2,1)S(1)} %get-tuple-element.57), channel_id=1, source_target_pairs={{0,56},{1,57},{2,58},{3,59},{4,60},{5,61},{6,62},{7,63},{8,32},{9,... | collective-permute-start | bytes 393224 | tf_op jit(solution)/shard_map/ppermute | solution.py:31
  130.4 5.2 %collective-permute-done.15.refs_2_ = bf16[32,2048]{1,0:T(8,128)(2,1)S(1)} collective-permute-done((bf16[32,2048]{1,0:T(8,128)(2,1)S(1)}, bf16[32,2048]{1,0:T(8,128)(2,1)S(1)}, u32[]{:S(2)}, u32[]{:S(2)}) %collective-permute-start.15) | collective-permute-done | bytes 131104 | tf_op jit(solution)/shard_map/ppermute | solution.py:31
  135.6 3.7 %collective-permute-done.16.refs_3_ = bf16[32,2048]{1,0:T(8,128)(2,1)S(1)} collective-permute-done((bf16[32,2048]{1,0:T(8,128)(2,1)S(1)}, bf16[32,2048]{1,0:T(8,128)(2,1)S(1)}, u32[]{:S(2)}, u32[]{:S(2)}) %collective-permute-start.16) | collective-permute-done | bytes 131104 | tf_op jit(solution)/shard_map/ppermute | solution.py:31
  139.9 2.4 %collective-permute-done.13.refs_1_ = bf16[32,2048]{1,0:T(8,128)(2,1)S(1)} collective-permute-done((bf16[32,2048]{1,0:T(8,128)(2,1)S(1)}, bf16[32,2048]{1,0:T(8,128)(2,1)S(1)}, u32[]{:S(2)}, u32[]{:S(2)}) %collective-permute-start.13) | collective-permute-done | bytes 131104 | tf_op jit(solution)/shard_map/ppermute | solution.py:31
  142.3 1.7 %shard_map.83 = bf16[256,2048]{1,0:T(8,128)(2,1)} custom-call(bf16[256,2048]{1,0:T(8,128)(2,1)S(1)} %collective-permute-done.7.tokens_ref, f32[128,256]{1,0:T(8,128)S(1)} %collective-permute-done.weight_ref, bf16[32,2048]{1,0:T(8,128)(2,1)S(1)} %collective-permute-done.12.refs_0_, bf16[32,2048]{1,0:T(8,128)(2,1)S(1)} %collective-permute-done.13.refs_1_, ...), custom_call_target="tpu_custom_call" | custom-call | tf_op jit(solution)/shard_map/pallas_call | solution.py:70
  (36 shorter events, 15.1 us)
Async XLA Ops:
  0.1 1.2 copy-start.2
  1.3 0.7 copy-start.7
  2.0 0.7 copy-start.8
  2.7 0.7 copy-start.9
  3.4 18.2 %copy-start.3 = (bf16[1,1,2048,192]{2,3,1,0:T(8,128)(2,1)S(1)}, bf16[1,1,2048,192]{2,3,1,0:T(8,128)(2,1)}, u32[]{:S(2)}) copy-start(bf16[1,1,2048,192]{2,3,1,0:T(8,128)(2,1)} %param.9) | copy-start | bytes 2359300
  3.4 20.1 %copy-start.5 = (bf16[1,1,2048,192]{2,3,1,0:T(8,128)(2,1)S(1)}, bf16[1,1,2048,192]{2,3,1,0:T(8,128)(2,1)}, u32[]{:S(2)}) copy-start(bf16[1,1,2048,192]{2,3,1,0:T(8,128)(2,1)} %param.10) | copy-start | bytes 2359300
  5.7 45.4 %all-to-all-start = ((bf16[8,32,2048]{2,1,0:T(8,128)(2,1)}), bf16[8,32,2048]{2,1,0:T(8,128)(2,1)}, u32[]{:S(2)}, u32[]{:S(2)}) async-start(bf16[8,32,2048]{2,1,0:T(8,128)(2,1)} %bitcast.7), calls=%async_computation | async-start | bytes 2097152 | tf_op jit(solution)/shard_map/all_to_all | solution.py:63
  21.6 12.3 %collective-permute-start.1 = (bf16[192,2048]{1,0:T(8,128)(2,1)S(1)}, bf16[192,2048]{1,0:T(8,128)(2,1)S(1)}, u32[]{:S(2)}, u32[]{:S(2)}) collective-permute-start(bf16[192,2048]{1,0:T(8,128)(2,1)S(1)} %bitcast.21), channel_id=1, source_target_pairs={{0,1},{1,0},{2,3},{3,2},{4,5},{5,4},{6,7},{7,6},{8,9},{9,8},{10,11... | collective-permute-start | bytes 2359304 | tf_op jit(solution)/shard_map/ppermute | solution.py:31
  23.5 10.3 %collective-permute-start.2 = (bf16[192,2048]{1,0:T(8,128)(2,1)S(1)}, bf16[192,2048]{1,0:T(8,128)(2,1)S(1)}, u32[]{:S(2)}, u32[]{:S(2)}) collective-permute-start(bf16[192,2048]{1,0:T(8,128)(2,1)S(1)} %bitcast.23), channel_id=1, source_target_pairs={{0,1},{1,0},{2,3},{3,2},{4,5},{5,4},{6,7},{7,6},{8,9},{9,8},{10,11... | collective-permute-start | bytes 2359304 | tf_op jit(solution)/shard_map/ppermute | solution.py:31
  25.9 7.9 %collective-permute-start.3 = (bf16[192,2048]{1,0:T(8,128)(2,1)}, bf16[192,2048]{1,0:T(8,128)(2,1)S(1)}, u32[]{:S(2)}, u32[]{:S(2)}) collective-permute-start(bf16[192,2048]{1,0:T(8,128)(2,1)} %bitcast.15.refs_4_), channel_id=1, source_target_pairs={{0,1},{1,0},{2,3},{3,2},{4,5},{5,4},{6,7},{7,6},{8,9},{9,8},{10,11... | collective-permute-start | bytes 2359304 | tf_op jit(solution)/shard_map/ppermute | solution.py:31
  27.8 35.6 %collective-permute-start.5 = (bf16[192,2048]{1,0:T(8,128)(2,1)}, bf16[192,2048]{1,0:T(8,128)(2,1)}, u32[]{:S(2)}, u32[]{:S(2)}) collective-permute-start(bf16[192,2048]{1,0:T(8,128)(2,1)} %bitcast.15.refs_4_), channel_id=1, source_target_pairs={{0,4},{1,5},{2,6},{3,7},{4,0},{5,1},{6,2},{7,3},{8,12},{9,13},{10,... | collective-permute-start | bytes 2359304 | tf_op jit(solution)/shard_map/ppermute | solution.py:31
  30.4 20.0 %collective-permute-start = (f32[128,256]{1,0:T(8,128)S(1)}, f32[128,256]{1,0:T(8,128)S(1)}, u32[]{:S(2)}, u32[]{:S(2)}) collective-permute-start(f32[128,256]{1,0:T(8,128)S(1)} %get-tuple-element.34), channel_id=1, source_target_pairs={{0,32},{1,33},{2,34},{3,35},{4,36},{5,37},{6,38},{7,39},{8,40},{9,... | collective-permute-start | bytes 393224 | tf_op jit(solution)/shard_map/ppermute | solution.py:31
  33.9 1.1 copy-start.4
  35.0 1.1 copy-start.6
  37.6 1.2 copy-start
  52.4 20.8 %collective-permute-start.4 = (bf16[128,2048]{1,0:T(8,128)(2,1)S(1)}, bf16[128,2048]{1,0:T(8,128)(2,1)S(1)}, u32[]{:S(2)}, u32[]{:S(2)}) collective-permute-start(bf16[128,2048]{1,0:T(8,128)(2,1)S(1)} %get-tuple-element.41.far_ref), channel_id=1, source_target_pairs={{0,4},{1,5},{2,6},{3,7},{4,0},{5,1},{6,2},{7,3},{8,12},{9,13},{10,... | collective-permute-start | bytes 1572872 | tf_op jit(solution)/shard_map/ppermute | solution.py:31
  58.0 29.8 %collective-permute-start.7 = (bf16[256,2048]{1,0:T(8,128)(2,1)}, bf16[256,2048]{1,0:T(8,128)(2,1)S(1)}, u32[]{:S(2)}, u32[]{:S(2)}) collective-permute-start(bf16[256,2048]{1,0:T(8,128)(2,1)} %bitcast.19), channel_id=1, source_target_pairs={{0,32},{1,33},{2,34},{3,35},{4,36},{5,37},{6,38},{7,39},{8,40},{9,... | collective-permute-start | bytes 3145736 | tf_op jit(solution)/shard_map/ppermute | solution.py:31
  60.0 1.4 copy-start.1
  73.2 5.4 %collective-permute-start.8 = (bf16[192,2048]{1,0:T(8,128)(2,1)}, bf16[192,2048]{1,0:T(8,128)(2,1)S(1)}, u32[]{:S(2)}, u32[]{:S(2)}) collective-permute-start(bf16[192,2048]{1,0:T(8,128)(2,1)} %collective-permute-done.5.refs_0_), channel_id=1, source_target_pairs={{0,1},{1,0},{2,3},{3,2},{4,5},{5,4},{6,7},{7,6},{8,9},{9,8},{10,11... | collective-permute-start | bytes 2359304 | tf_op jit(solution)/shard_map/ppermute | solution.py:31
  76.2 7.1 %collective-permute-start.6 = (bf16[128,384]{1,0:T(8,128)(2,1)S(1)}, bf16[128,384]{1,0:T(8,128)(2,1)S(1)}, u32[]{:S(2)}, u32[]{:S(2)}) collective-permute-start(bf16[128,384]{1,0:T(8,128)(2,1)S(1)} %shard_map.77), channel_id=1, source_target_pairs={{0,4},{1,5},{2,6},{3,7},{4,0},{5,1},{6,2},{7,3},{8,12},{9,13},{10,... | collective-permute-start | bytes 294920 | tf_op jit(solution)/shard_map/ppermute | solution.py:31
  87.8 13.5 %collective-permute-start.9 = (bf16[128,2048]{1,0:T(8,128)(2,1)S(1)}, bf16[128,2048]{1,0:T(8,128)(2,1)S(1)}, u32[]{:S(2)}, u32[]{:S(2)}) collective-permute-start(bf16[128,2048]{1,0:T(8,128)(2,1)S(1)} %get-tuple-element.52.near_ref), channel_id=1, source_target_pairs={{0,4},{1,5},{2,6},{3,7},{4,0},{5,1},{6,2},{7,3},{8,12},{9,13},{10,... | collective-permute-start | bytes 1572872 | tf_op jit(solution)/shard_map/ppermute | solution.py:31
  90.4 25.7 %collective-permute-start.14 = (bf16[64,2048]{1,0:T(8,128)(2,1)S(1)}, bf16[64,2048]{1,0:T(8,128)(2,1)S(1)}, u32[]{:S(2)}, u32[]{:S(2)}) collective-permute-start(bf16[64,2048]{1,0:T(8,128)(2,1)S(1)} %get-tuple-element.58), channel_id=1, source_target_pairs={{0,2},{1,3},{2,0},{3,1},{4,6},{5,7},{6,4},{7,5},{8,10},{9,11},{10,... | collective-permute-start | bytes 786440 | tf_op jit(solution)/shard_map/ppermute | solution.py:31
  98.5 25.1 %collective-permute-start.11 = (bf16[64,2048]{1,0:T(8,128)(2,1)S(1)}, bf16[64,2048]{1,0:T(8,128)(2,1)S(1)}, u32[]{:S(2)}, u32[]{:S(2)}) collective-permute-start(bf16[64,2048]{1,0:T(8,128)(2,1)S(1)} %get-tuple-element.55), channel_id=1, source_target_pairs={{0,2},{1,3},{2,0},{3,1},{4,6},{5,7},{6,4},{7,5},{8,10},{9,11},{10,... | collective-permute-start | bytes 786440 | tf_op jit(solution)/shard_map/ppermute | solution.py:31
  102.3 13.8 %collective-permute-start.10 = (bf16[128,384]{1,0:T(8,128)(2,1)S(1)}, bf16[128,384]{1,0:T(8,128)(2,1)S(1)}, u32[]{:S(2)}, u32[]{:S(2)}) collective-permute-start(bf16[128,384]{1,0:T(8,128)(2,1)S(1)} %shard_map.79), channel_id=1, source_target_pairs={{0,4},{1,5},{2,6},{3,7},{4,0},{5,1},{6,2},{7,3},{8,12},{9,13},{10,... | collective-permute-start | bytes 294920 | tf_op jit(solution)/shard_map/ppermute | solution.py:31
  116.5 19.0 %collective-permute-start.15 = (bf16[32,2048]{1,0:T(8,128)(2,1)S(1)}, bf16[32,2048]{1,0:T(8,128)(2,1)S(1)}, u32[]{:S(2)}, u32[]{:S(2)}) collective-permute-start(bf16[32,2048]{1,0:T(8,128)(2,1)S(1)} %get-tuple-element.59), channel_id=1, source_target_pairs={{0,48},{1,49},{2,50},{3,51},{4,52},{5,53},{6,54},{7,55},{8,56},{9,... | collective-permute-start | bytes 393224 | tf_op jit(solution)/shard_map/ppermute | solution.py:31
  118.5 20.8 %collective-permute-start.16 = (bf16[32,2048]{1,0:T(8,128)(2,1)S(1)}, bf16[32,2048]{1,0:T(8,128)(2,1)S(1)}, u32[]{:S(2)}, u32[]{:S(2)}) collective-permute-start(bf16[32,2048]{1,0:T(8,128)(2,1)S(1)} %get-tuple-element.60), channel_id=1, source_target_pairs={{0,40},{1,41},{2,42},{3,43},{4,44},{5,45},{6,46},{7,47},{8,48},{9,... | collective-permute-start | bytes 393224 | tf_op jit(solution)/shard_map/ppermute | solution.py:31
  124.0 15.9 %collective-permute-start.12 = (bf16[32,2048]{1,0:T(8,128)(2,1)S(1)}, bf16[32,2048]{1,0:T(8,128)(2,1)S(1)}, u32[]{:S(2)}, u32[]{:S(2)}) collective-permute-start(bf16[32,2048]{1,0:T(8,128)(2,1)S(1)} %get-tuple-element.56), channel_id=1, source_target_pairs={{0,32},{1,33},{2,34},{3,35},{4,36},{5,37},{6,38},{7,39},{8,40},{9,... | collective-permute-start | bytes 393224 | tf_op jit(solution)/shard_map/ppermute | solution.py:31
  126.0 16.4 %collective-permute-start.13 = (bf16[32,2048]{1,0:T(8,128)(2,1)S(1)}, bf16[32,2048]{1,0:T(8,128)(2,1)S(1)}, u32[]{:S(2)}, u32[]{:S(2)}) collective-permute-start(bf16[32,2048]{1,0:T(8,128)(2,1)S(1)} %get-tuple-element.57), channel_id=1, source_target_pairs={{0,56},{1,57},{2,58},{3,59},{4,60},{5,61},{6,62},{7,63},{8,32},{9,... | collective-permute-start | bytes 393224 | tf_op jit(solution)/shard_map/ppermute | solution.py:31

commit v3 on v2

--- a/solution.py
+++ b/solution.py
@@ -66,13 +66,13 @@
     return parts.reshape(x.shape)
 
 
-def called(kernel, out_shape, *xs, scalars=0):
+def called(kernel, out_shape, *xs, scalars=0, room=ROOM):
     return pl.pallas_call(
         kernel,
         out_shape=out_shape,
         in_specs=[pl.BlockSpec(memory_space=pltpu.SMEM)] * scalars + [VMEM] * (len(xs) - scalars),
         out_specs=jax.tree.map(lambda _: VMEM, out_shape),
-        compiler_params=pltpu.CompilerParams(vmem_limit_bytes=ROOM),
+        compiler_params=pltpu.CompilerParams(vmem_limit_bytes=room),
         cost_estimate=pl.CostEstimate(flops=0, bytes_accessed=0, transcendentals=0),
     )(*xs)
 
@@ -201,6 +201,7 @@
         routes[0].T,
         mixing[0].T,
         scalars=1,
+        room=60 * 1024 * 1024,
     )
 
     pairs = ((gate, other_core(gate)), (up, other_core(up)), (down, other_core(down)))

time: 145 us -> 143 us (0.986)
  the two profiles are of different devices: /device:TPU:16 before, /device:TPU:24 now
where the time goes in v3:
time: 143 us; the launch traced here: 142 us
  starting transfers between devices  67 us (47%)
  waiting for transfers between devices  54.9 us (38%)
  Pallas kernels  14.1 us (10%)
  local copies, waits for them, and re-layouts  4.86 us (3%)
    ppermute x17, waiting for transfers between devices, permuted(): return lax.ppermute(x, 'ep' if sections == 1 else ('pp', 'ep'), pairs)  53.8 us
    ppermute x17, starting transfers between devices, permuted(): return lax.ppermute(x, 'ep' if sections == 1 else ('pp', 'ep'), pairs)  51.9 us
    all_to_all x1, starting transfers between devices, exchanged(): lax.all_to_all(parts, 'ep', split_axis=0, concat_axis=0, axis_index_group...  15.1 us
    pallas_call x11, Pallas kernels, called(): pl.pallas_call(kernel, out_shape=out_shape, in_specs=[pl.BlockSpec(memory...  14.1 us
    unnamed x16, local copies, waits for them, and re-layouts  4.86 us
  transfers between devices with their start and end apart: 18, of which 10 were waited for; matrix products, arithmetic and copies ran while one was open for 0% of the time, Pallas kernels for 7%

profile of v3, /device:TPU:24, one launch (start us, length us, event | category | flops | bytes accessed | tf_op | source)
XLA Modules:
  0.0 141.8 jit_solution(14960944557071556305)
XLA Ops:
  0.6 3.1 %shard_map.73 = (bf16[256,2048]{1,0:T(8,128)(2,1)}, f32[128,256]{1,0:T(8,128)}) custom-call(s32[2]{0:T(128)} %pad_add_fusion.place_ref, bf16[256,2048]{1,0:T(8,128)(2,1)} %bitcast.23, bf16[1,2048]{1,0:T(2,128)(2,1)} %gain_ref.1, s32[8,256]{1,0:T(8,128)} %bitcast.26, f32[8,256]{1,0:T(8,128)} %bitcast.27), custom_call_target="tpu_custom_call" | custom-call | tf_op jit(solution)/shard_map/pallas_call | solution.py:70
  3.7 15.1 %all-to-all-start = ((bf16[8,32,2048]{2,1,0:T(8,128)(2,1)}), bf16[8,32,2048]{2,1,0:T(8,128)(2,1)}, u32[]{:S(2)}, u32[]{:S(2)}) async-start(bf16[8,32,2048]{2,1,0:T(8,128)(2,1)} %bitcast.25), calls=%async_computation | async-start | bytes 2097152 | tf_op jit(solution)/shard_map/all_to_all | solution.py:63
  18.9 1.9 %collective-permute-start.1 = (bf16[192,2048]{1,0:T(8,128)(2,1)S(1)}, bf16[192,2048]{1,0:T(8,128)(2,1)S(1)}, u32[]{:S(2)}, u32[]{:S(2)}) collective-permute-start(bf16[192,2048]{1,0:T(8,128)(2,1)S(1)} %bitcast.19), channel_id=1, source_target_pairs={{0,1},{1,0},{2,3},{3,2},{4,5},{5,4},{6,7},{7,6},{8,9},{9,8},{10,11... | collective-permute-start | bytes 2359304 | tf_op jit(solution)/shard_map/ppermute | solution.py:31
  20.8 2.4 %collective-permute-start.2 = (bf16[192,2048]{1,0:T(8,128)(2,1)S(1)}, bf16[192,2048]{1,0:T(8,128)(2,1)S(1)}, u32[]{:S(2)}, u32[]{:S(2)}) collective-permute-start(bf16[192,2048]{1,0:T(8,128)(2,1)S(1)} %bitcast.21), channel_id=1, source_target_pairs={{0,1},{1,0},{2,3},{3,2},{4,5},{5,4},{6,7},{7,6},{8,9},{9,8},{10,11... | collective-permute-start | bytes 2359304 | tf_op jit(solution)/shard_map/ppermute | solution.py:31
  23.2 1.9 %collective-permute-start.3 = (bf16[192,2048]{1,0:T(8,128)(2,1)}, bf16[192,2048]{1,0:T(8,128)(2,1)S(1)}, u32[]{:S(2)}, u32[]{:S(2)}) collective-permute-start(bf16[192,2048]{1,0:T(8,128)(2,1)} %bitcast.15.refs_4_), channel_id=1, source_target_pairs={{0,1},{1,0},{2,3},{3,2},{4,5},{5,4},{6,7},{7,6},{8,9},{9,8},{10,11... | collective-permute-start | bytes 2359304 | tf_op jit(solution)/shard_map/ppermute | solution.py:31
  25.1 3.3 %collective-permute-start.5 = (bf16[192,2048]{1,0:T(8,128)(2,1)}, bf16[192,2048]{1,0:T(8,128)(2,1)}, u32[]{:S(2)}, u32[]{:S(2)}) collective-permute-start(bf16[192,2048]{1,0:T(8,128)(2,1)} %bitcast.15.refs_4_), channel_id=1, source_target_pairs={{0,4},{1,5},{2,6},{3,7},{4,0},{5,1},{6,2},{7,3},{8,12},{9,13},{10,... | collective-permute-start | bytes 2359304 | tf_op jit(solution)/shard_map/ppermute | solution.py:31
  28.4 3.4 %collective-permute-start = (f32[128,256]{1,0:T(8,128)S(1)}, f32[128,256]{1,0:T(8,128)S(1)}, u32[]{:S(2)}, u32[]{:S(2)}) collective-permute-start(f32[128,256]{1,0:T(8,128)S(1)} %copy-done.7), channel_id=1, source_target_pairs={{0,32},{1,33},{2,34},{3,35},{4,36},{5,37},{6,38},{7,39},{8,40},{9,... | collective-permute-start | bytes 393224 | tf_op jit(solution)/shard_map/ppermute | solution.py:31
  34.1 1.4 %shard_map.74 = (bf16[384,2048]{1,0:T(8,128)(2,1)S(1)}, bf16[384,2048]{1,0:T(8,128)(2,1)S(1)}, bf16[384,2048]{1,0:T(8,128)(2,1)S(1)}) custom-call(bf16[192,2048]{1,0:T(8,128)(2,1)S(1)} %bitcast.20, bf16[192,2048]{1,0:T(8,128)(2,1)S(1)} %collective-permute-done.1.refs_1_, bf16[192,2048]{1,0:T(8,128)(2,1)S(1)} %bitcast.22, ...), custom_call_target="tpu_custom_call" | custom-call | tf_op jit(solution)/shard_map/pallas_call | solution.py:70
  36.7 13.7 %collective-permute-done.weight_ref = f32[128,256]{1,0:T(8,128)S(1)} collective-permute-done((f32[128,256]{1,0:T(8,128)S(1)}, f32[128,256]{1,0:T(8,128)S(1)}, u32[]{:S(2)}, u32[]{:S(2)}) %collective-permute-start) | collective-permute-done | bytes 131104 | tf_op jit(solution)/shard_map/ppermute | solution.py:31
  51.6 1.3 shard_map.75
  52.9 1.9 %collective-permute-start.4 = (bf16[128,2048]{1,0:T(8,128)(2,1)S(1)}, bf16[128,2048]{1,0:T(8,128)(2,1)S(1)}, u32[]{:S(2)}, u32[]{:S(2)}) collective-permute-start(bf16[128,2048]{1,0:T(8,128)(2,1)S(1)} %get-tuple-element.41.far_ref), channel_id=1, source_target_pairs={{0,4},{1,5},{2,6},{3,7},{4,0},{5,1},{6,2},{7,3},{8,12},{9,13},{10,... | collective-permute-start | bytes 1572872 | tf_op jit(solution)/shard_map/ppermute | solution.py:31
  54.9 3.6 %collective-permute-start.7 = (bf16[256,2048]{1,0:T(8,128)(2,1)}, bf16[256,2048]{1,0:T(8,128)(2,1)S(1)}, u32[]{:S(2)}, u32[]{:S(2)}) collective-permute-start(bf16[256,2048]{1,0:T(8,128)(2,1)} %bitcast.24), channel_id=1, source_target_pairs={{0,32},{1,33},{2,34},{3,35},{4,36},{5,37},{6,38},{7,39},{8,40},{9,... | collective-permute-start | bytes 3145736 | tf_op jit(solution)/shard_map/ppermute | solution.py:31
  58.5 1.4 copy-done.1
  59.9 1.9 %shard_map.76.mine_ref = f32[256,2048]{1,0:T(8,128)S(1)} custom-call(bf16[128,2048]{1,0:T(8,128)(2,1)S(1)} %get-tuple-element.41.far_ref, bf16[128,2048]{1,0:T(8,128)(2,1)S(1)} %get-tuple-element.52.near_ref, bf16[384,2048]{1,0:T(8,128)(2,1)S(1)} %get-tuple-element.43.gates, bf16[384,2048]{1,0:T(8,128)(2,1)S(1)} %get-tuple-element.44.ups, ...), custom_call_target="tpu_custom_call" | custom-call | tf_op jit(solution)/shard_map/pallas_call | solution.py:70
  61.8 8.5 %collective-permute-done.4.rows_ref = bf16[128,2048]{1,0:T(8,128)(2,1)S(1)} collective-permute-done((bf16[128,2048]{1,0:T(8,128)(2,1)S(1)}, bf16[128,2048]{1,0:T(8,128)(2,1)S(1)}, u32[]{:S(2)}, u32[]{:S(2)}) %collective-permute-start.4) | collective-permute-done | bytes 524320 | tf_op jit(solution)/shard_map/ppermute | solution.py:31
  70.3 1.9 %collective-permute-start.8 = (bf16[192,2048]{1,0:T(8,128)(2,1)}, bf16[192,2048]{1,0:T(8,128)(2,1)S(1)}, u32[]{:S(2)}, u32[]{:S(2)}) collective-permute-start(bf16[192,2048]{1,0:T(8,128)(2,1)} %collective-permute-done.5.refs_0_), channel_id=1, source_target_pairs={{0,1},{1,0},{2,3},{3,2},{4,5},{5,4},{6,7},{7,6},{8,9},{9,8},{10,11... | collective-permute-start | bytes 2359304 | tf_op jit(solution)/shard_map/ppermute | solution.py:31
  73.2 3.5 %collective-permute-start.6 = (bf16[128,384]{1,0:T(8,128)(2,1)S(1)}, bf16[128,384]{1,0:T(8,128)(2,1)S(1)}, u32[]{:S(2)}, u32[]{:S(2)}) collective-permute-start(bf16[128,384]{1,0:T(8,128)(2,1)S(1)} %shard_map.77), channel_id=1, source_target_pairs={{0,4},{1,5},{2,6},{3,7},{4,0},{5,1},{6,2},{7,3},{8,12},{9,13},{10,... | collective-permute-start | bytes 294920 | tf_op jit(solution)/shard_map/ppermute | solution.py:31
  78.0 2.4 %collective-permute-done.6.hidden_ref = bf16[128,384]{1,0:T(8,128)(2,1)S(1)} collective-permute-done((bf16[128,384]{1,0:T(8,128)(2,1)S(1)}, bf16[128,384]{1,0:T(8,128)(2,1)S(1)}, u32[]{:S(2)}, u32[]{:S(2)}) %collective-permute-start.6) | collective-permute-done | bytes 98336 | tf_op jit(solution)/shard_map/ppermute | solution.py:31
  80.3 4.4 %collective-permute-done.7.tokens_ref = bf16[256,2048]{1,0:T(8,128)(2,1)S(1)} collective-permute-done((bf16[256,2048]{1,0:T(8,128)(2,1)}, bf16[256,2048]{1,0:T(8,128)(2,1)S(1)}, u32[]{:S(2)}, u32[]{:S(2)}) %collective-permute-start.7) | collective-permute-done | bytes 1048608 | tf_op jit(solution)/shard_map/ppermute | solution.py:31
  84.7 3.6 %collective-permute-start.9 = (bf16[128,2048]{1,0:T(8,128)(2,1)S(1)}, bf16[128,2048]{1,0:T(8,128)(2,1)S(1)}, u32[]{:S(2)}, u32[]{:S(2)}) collective-permute-start(bf16[128,2048]{1,0:T(8,128)(2,1)S(1)} %get-tuple-element.52.near_ref), channel_id=1, source_target_pairs={{0,4},{1,5},{2,6},{3,7},{4,0},{5,1},{6,2},{7,3},{8,12},{9,13},{10,... | collective-permute-start | bytes 1572872 | tf_op jit(solution)/shard_map/ppermute | solution.py:31
  88.8 8.0 %collective-permute-start.14 = (bf16[64,2048]{1,0:T(8,128)(2,1)S(1)}, bf16[64,2048]{1,0:T(8,128)(2,1)S(1)}, u32[]{:S(2)}, u32[]{:S(2)}) collective-permute-start(bf16[64,2048]{1,0:T(8,128)(2,1)S(1)} %get-tuple-element.58), channel_id=1, source_target_pairs={{0,2},{1,3},{2,0},{3,1},{4,6},{5,7},{6,4},{7,5},{8,10},{9,11},{10,... | collective-permute-start | bytes 786440 | tf_op jit(solution)/shard_map/ppermute | solution.py:31
  96.8 1.9 %collective-permute-start.11 = (bf16[64,2048]{1,0:T(8,128)(2,1)S(1)}, bf16[64,2048]{1,0:T(8,128)(2,1)S(1)}, u32[]{:S(2)}, u32[]{:S(2)}) collective-permute-start(bf16[64,2048]{1,0:T(8,128)(2,1)S(1)} %get-tuple-element.55), channel_id=1, source_target_pairs={{0,2},{1,3},{2,0},{3,1},{4,6},{5,7},{6,4},{7,5},{8,10},{9,11},{10,... | collective-permute-start | bytes 786440 | tf_op jit(solution)/shard_map/ppermute | solution.py:31
  99.8 2.8 %collective-permute-start.10 = (bf16[128,384]{1,0:T(8,128)(2,1)S(1)}, bf16[128,384]{1,0:T(8,128)(2,1)S(1)}, u32[]{:S(2)}, u32[]{:S(2)}) collective-permute-start(bf16[128,384]{1,0:T(8,128)(2,1)S(1)} %shard_map.79), channel_id=1, source_target_pairs={{0,4},{1,5},{2,6},{3,7},{4,0},{5,1},{6,2},{7,3},{8,12},{9,13},{10,... | collective-permute-start | bytes 294920 | tf_op jit(solution)/shard_map/ppermute | solution.py:31
  102.7 11.8 %collective-permute-done.14.refs_0_ = bf16[64,2048]{1,0:T(8,128)(2,1)S(1)} collective-permute-done((bf16[64,2048]{1,0:T(8,128)(2,1)S(1)}, bf16[64,2048]{1,0:T(8,128)(2,1)S(1)}, u32[]{:S(2)}, u32[]{:S(2)}) %collective-permute-start.14) | collective-permute-done | bytes 262176 | tf_op jit(solution)/shard_map/ppermute | solution.py:31
  114.9 1.9 %collective-permute-start.15 = (bf16[32,2048]{1,0:T(8,128)(2,1)S(1)}, bf16[32,2048]{1,0:T(8,128)(2,1)S(1)}, u32[]{:S(2)}, u32[]{:S(2)}) collective-permute-start(bf16[32,2048]{1,0:T(8,128)(2,1)S(1)} %get-tuple-element.59), channel_id=1, source_target_pairs={{0,48},{1,49},{2,50},{3,51},{4,52},{5,53},{6,54},{7,55},{8,56},{9,... | collective-permute-start | bytes 393224 | tf_op jit(solution)/shard_map/ppermute | solution.py:31
  116.8 1.9 %collective-permute-start.16 = (bf16[32,2048]{1,0:T(8,128)(2,1)S(1)}, bf16[32,2048]{1,0:T(8,128)(2,1)S(1)}, u32[]{:S(2)}, u32[]{:S(2)}) collective-permute-start(bf16[32,2048]{1,0:T(8,128)(2,1)S(1)} %get-tuple-element.60), channel_id=1, source_target_pairs={{0,40},{1,41},{2,42},{3,43},{4,44},{5,45},{6,46},{7,47},{8,48},{9,... | collective-permute-start | bytes 393224 | tf_op jit(solution)/shard_map/ppermute | solution.py:31
  118.7 1.6 %collective-permute-done.11.refs_0_ = bf16[64,2048]{1,0:T(8,128)(2,1)S(1)} collective-permute-done((bf16[64,2048]{1,0:T(8,128)(2,1)S(1)}, bf16[64,2048]{1,0:T(8,128)(2,1)S(1)}, u32[]{:S(2)}, u32[]{:S(2)}) %collective-permute-start.11) | collective-permute-done | bytes 262176 | tf_op jit(solution)/shard_map/ppermute | solution.py:31
  120.7 1.9 %collective-permute-start.12 = (bf16[32,2048]{1,0:T(8,128)(2,1)S(1)}, bf16[32,2048]{1,0:T(8,128)(2,1)S(1)}, u32[]{:S(2)}, u32[]{:S(2)}) collective-permute-start(bf16[32,2048]{1,0:T(8,128)(2,1)S(1)} %get-tuple-element.56), channel_id=1, source_target_pairs={{0,32},{1,33},{2,34},{3,35},{4,36},{5,37},{6,38},{7,39},{8,40},{9,... | collective-permute-start | bytes 393224 | tf_op jit(solution)/shard_map/ppermute | solution.py:31
  122.7 5.9 %collective-permute-start.13 = (bf16[32,2048]{1,0:T(8,128)(2,1)S(1)}, bf16[32,2048]{1,0:T(8,128)(2,1)S(1)}, u32[]{:S(2)}, u32[]{:S(2)}) collective-permute-start(bf16[32,2048]{1,0:T(8,128)(2,1)S(1)} %get-tuple-element.57), channel_id=1, source_target_pairs={{0,56},{1,57},{2,58},{3,59},{4,60},{5,61},{6,62},{7,63},{8,32},{9,... | collective-permute-start | bytes 393224 | tf_op jit(solution)/shard_map/ppermute | solution.py:31
  128.6 4.8 %collective-permute-done.15.refs_2_ = bf16[32,2048]{1,0:T(8,128)(2,1)S(1)} collective-permute-done((bf16[32,2048]{1,0:T(8,128)(2,1)S(1)}, bf16[32,2048]{1,0:T(8,128)(2,1)S(1)}, u32[]{:S(2)}, u32[]{:S(2)}) %collective-permute-start.15) | collective-permute-done | bytes 131104 | tf_op jit(solution)/shard_map/ppermute | solution.py:31
  133.4 6.2 %collective-permute-done.16.refs_3_ = bf16[32,2048]{1,0:T(8,128)(2,1)S(1)} collective-permute-done((bf16[32,2048]{1,0:T(8,128)(2,1)S(1)}, bf16[32,2048]{1,0:T(8,128)(2,1)S(1)}, u32[]{:S(2)}, u32[]{:S(2)}) %collective-permute-start.16) | collective-permute-done | bytes 131104 | tf_op jit(solution)/shard_map/ppermute | solution.py:31
  140.1 1.7 %shard_map.83 = bf16[256,2048]{1,0:T(8,128)(2,1)} custom-call(bf16[256,2048]{1,0:T(8,128)(2,1)S(1)} %collective-permute-done.7.tokens_ref, f32[128,256]{1,0:T(8,128)S(1)} %collective-permute-done.weight_ref, bf16[32,2048]{1,0:T(8,128)(2,1)S(1)} %collective-permute-done.12.refs_0_, bf16[32,2048]{1,0:T(8,128)(2,1)S(1)} %collective-permute-done.13.refs_1_, ...), custom_call_target="tpu_custom_call" | custom-call | tf_op jit(solution)/shard_map/pallas_call | solution.py:70
  (32 shorter events, 10.3 us)
Async XLA Ops:
  0.6 18.2 %copy-start.2 = (bf16[1,1,2048,192]{2,3,1,0:T(8,128)(2,1)S(1)}, bf16[1,1,2048,192]{2,3,1,0:T(8,128)(2,1)}, u32[]{:S(2)}) copy-start(bf16[1,1,2048,192]{2,3,1,0:T(8,128)(2,1)} %param.9) | copy-start | bytes 2359300
  0.6 20.2 %copy-start.4 = (bf16[1,1,2048,192]{2,3,1,0:T(8,128)(2,1)S(1)}, bf16[1,1,2048,192]{2,3,1,0:T(8,128)(2,1)}, u32[]{:S(2)}) copy-start(bf16[1,1,2048,192]{2,3,1,0:T(8,128)(2,1)} %param.10) | copy-start | bytes 2359300
  3.7 24.7 %copy-start.7 = (f32[128,256]{1,0:T(8,128)S(1)}, f32[128,256]{1,0:T(8,128)}, u32[]{:S(2)}) copy-start(f32[128,256]{1,0:T(8,128)} %get-tuple-element.34) | copy-start | bytes 393220
  3.7 47.9 %all-to-all-start = ((bf16[8,32,2048]{2,1,0:T(8,128)(2,1)}), bf16[8,32,2048]{2,1,0:T(8,128)(2,1)}, u32[]{:S(2)}, u32[]{:S(2)}) async-start(bf16[8,32,2048]{2,1,0:T(8,128)(2,1)} %bitcast.25), calls=%async_computation | async-start | bytes 2097152 | tf_op jit(solution)/shard_map/all_to_all | solution.py:63
  18.9 13.0 %collective-permute-start.1 = (bf16[192,2048]{1,0:T(8,128)(2,1)S(1)}, bf16[192,2048]{1,0:T(8,128)(2,1)S(1)}, u32[]{:S(2)}, u32[]{:S(2)}) collective-permute-start(bf16[192,2048]{1,0:T(8,128)(2,1)S(1)} %bitcast.19), channel_id=1, source_target_pairs={{0,1},{1,0},{2,3},{3,2},{4,5},{5,4},{6,7},{7,6},{8,9},{9,8},{10,11... | collective-permute-start | bytes 2359304 | tf_op jit(solution)/shard_map/ppermute | solution.py:31
  20.8 11.0 %collective-permute-start.2 = (bf16[192,2048]{1,0:T(8,128)(2,1)S(1)}, bf16[192,2048]{1,0:T(8,128)(2,1)S(1)}, u32[]{:S(2)}, u32[]{:S(2)}) collective-permute-start(bf16[192,2048]{1,0:T(8,128)(2,1)S(1)} %bitcast.21), channel_id=1, source_target_pairs={{0,1},{1,0},{2,3},{3,2},{4,5},{5,4},{6,7},{7,6},{8,9},{9,8},{10,11... | collective-permute-start | bytes 2359304 | tf_op jit(solution)/shard_map/ppermute | solution.py:31
  23.2 8.6 %collective-permute-start.3 = (bf16[192,2048]{1,0:T(8,128)(2,1)}, bf16[192,2048]{1,0:T(8,128)(2,1)S(1)}, u32[]{:S(2)}, u32[]{:S(2)}) collective-permute-start(bf16[192,2048]{1,0:T(8,128)(2,1)} %bitcast.15.refs_4_), channel_id=1, source_target_pairs={{0,1},{1,0},{2,3},{3,2},{4,5},{5,4},{6,7},{7,6},{8,9},{9,8},{10,11... | collective-permute-start | bytes 2359304 | tf_op jit(solution)/shard_map/ppermute | solution.py:31
  25.1 36.7 %collective-permute-start.5 = (bf16[192,2048]{1,0:T(8,128)(2,1)}, bf16[192,2048]{1,0:T(8,128)(2,1)}, u32[]{:S(2)}, u32[]{:S(2)}) collective-permute-start(bf16[192,2048]{1,0:T(8,128)(2,1)} %bitcast.15.refs_4_), channel_id=1, source_target_pairs={{0,4},{1,5},{2,6},{3,7},{4,0},{5,1},{6,2},{7,3},{8,12},{9,13},{10,... | collective-permute-start | bytes 2359304 | tf_op jit(solution)/shard_map/ppermute | solution.py:31
  28.4 23.2 %copy-start.6 = (s32[2]{0:T(128)S(1)}, s32[2]{0:T(128)}, u32[]{:S(2)}) copy-start(s32[2]{0:T(128)} %pad_add_fusion.place_ref) | copy-start | bytes 28
  28.4 22.0 %collective-permute-start = (f32[128,256]{1,0:T(8,128)S(1)}, f32[128,256]{1,0:T(8,128)S(1)}, u32[]{:S(2)}, u32[]{:S(2)}) collective-permute-start(f32[128,256]{1,0:T(8,128)S(1)} %copy-done.7), channel_id=1, source_target_pairs={{0,32},{1,33},{2,34},{3,35},{4,36},{5,37},{6,38},{7,39},{8,40},{9,... | collective-permute-start | bytes 393224 | tf_op jit(solution)/shard_map/ppermute | solution.py:31
  31.8 1.1 copy-start.3
  33.0 1.1 copy-start.5
  35.6 1.2 copy-start
  52.9 17.3 %collective-permute-start.4 = (bf16[128,2048]{1,0:T(8,128)(2,1)S(1)}, bf16[128,2048]{1,0:T(8,128)(2,1)S(1)}, u32[]{:S(2)}, u32[]{:S(2)}) collective-permute-start(bf16[128,2048]{1,0:T(8,128)(2,1)S(1)} %get-tuple-element.41.far_ref), channel_id=1, source_target_pairs={{0,4},{1,5},{2,6},{3,7},{4,0},{5,1},{6,2},{7,3},{8,12},{9,13},{10,... | collective-permute-start | bytes 1572872 | tf_op jit(solution)/shard_map/ppermute | solution.py:31
  54.9 29.8 %collective-permute-start.7 = (bf16[256,2048]{1,0:T(8,128)(2,1)}, bf16[256,2048]{1,0:T(8,128)(2,1)S(1)}, u32[]{:S(2)}, u32[]{:S(2)}) collective-permute-start(bf16[256,2048]{1,0:T(8,128)(2,1)} %bitcast.24), channel_id=1, source_target_pairs={{0,32},{1,33},{2,34},{3,35},{4,36},{5,37},{6,38},{7,39},{8,40},{9,... | collective-permute-start | bytes 3145736 | tf_op jit(solution)/shard_map/ppermute | solution.py:31
  58.5 1.4 copy-start.1
  70.3 6.5 %collective-permute-start.8 = (bf16[192,2048]{1,0:T(8,128)(2,1)}, bf16[192,2048]{1,0:T(8,128)(2,1)S(1)}, u32[]{:S(2)}, u32[]{:S(2)}) collective-permute-start(bf16[192,2048]{1,0:T(8,128)(2,1)} %collective-permute-done.5.refs_0_), channel_id=1, source_target_pairs={{0,1},{1,0},{2,3},{3,2},{4,5},{5,4},{6,7},{7,6},{8,9},{9,8},{10,11... | collective-permute-start | bytes 2359304 | tf_op jit(solution)/shard_map/ppermute | solution.py:31
  73.2 7.1 %collective-permute-start.6 = (bf16[128,384]{1,0:T(8,128)(2,1)S(1)}, bf16[128,384]{1,0:T(8,128)(2,1)S(1)}, u32[]{:S(2)}, u32[]{:S(2)}) collective-permute-start(bf16[128,384]{1,0:T(8,128)(2,1)S(1)} %shard_map.77), channel_id=1, source_target_pairs={{0,4},{1,5},{2,6},{3,7},{4,0},{5,1},{6,2},{7,3},{8,12},{9,13},{10,... | collective-permute-start | bytes 294920 | tf_op jit(solution)/shard_map/ppermute | solution.py:31
  84.7 14.1 %collective-permute-start.9 = (bf16[128,2048]{1,0:T(8,128)(2,1)S(1)}, bf16[128,2048]{1,0:T(8,128)(2,1)S(1)}, u32[]{:S(2)}, u32[]{:S(2)}) collective-permute-start(bf16[128,2048]{1,0:T(8,128)(2,1)S(1)} %get-tuple-element.52.near_ref), channel_id=1, source_target_pairs={{0,4},{1,5},{2,6},{3,7},{4,0},{5,1},{6,2},{7,3},{8,12},{9,13},{10,... | collective-permute-start | bytes 1572872 | tf_op jit(solution)/shard_map/ppermute | solution.py:31
  88.8 25.7 %collective-permute-start.14 = (bf16[64,2048]{1,0:T(8,128)(2,1)S(1)}, bf16[64,2048]{1,0:T(8,128)(2,1)S(1)}, u32[]{:S(2)}, u32[]{:S(2)}) collective-permute-start(bf16[64,2048]{1,0:T(8,128)(2,1)S(1)} %get-tuple-element.58), channel_id=1, source_target_pairs={{0,2},{1,3},{2,0},{3,1},{4,6},{5,7},{6,4},{7,5},{8,10},{9,11},{10,... | collective-permute-start | bytes 786440 | tf_op jit(solution)/shard_map/ppermute | solution.py:31
  96.8 23.5 %collective-permute-start.11 = (bf16[64,2048]{1,0:T(8,128)(2,1)S(1)}, bf16[64,2048]{1,0:T(8,128)(2,1)S(1)}, u32[]{:S(2)}, u32[]{:S(2)}) collective-permute-start(bf16[64,2048]{1,0:T(8,128)(2,1)S(1)} %get-tuple-element.55), channel_id=1, source_target_pairs={{0,2},{1,3},{2,0},{3,1},{4,6},{5,7},{6,4},{7,5},{8,10},{9,11},{10,... | collective-permute-start | bytes 786440 | tf_op jit(solution)/shard_map/ppermute | solution.py:31
  99.8 14.6 %collective-permute-start.10 = (bf16[128,384]{1,0:T(8,128)(2,1)S(1)}, bf16[128,384]{1,0:T(8,128)(2,1)S(1)}, u32[]{:S(2)}, u32[]{:S(2)}) collective-permute-start(bf16[128,384]{1,0:T(8,128)(2,1)S(1)} %shard_map.79), channel_id=1, source_target_pairs={{0,4},{1,5},{2,6},{3,7},{4,0},{5,1},{6,2},{7,3},{8,12},{9,13},{10,... | collective-permute-start | bytes 294920 | tf_op jit(solution)/shard_map/ppermute | solution.py:31
  114.9 18.5 %collective-permute-start.15 = (bf16[32,2048]{1,0:T(8,128)(2,1)S(1)}, bf16[32,2048]{1,0:T(8,128)(2,1)S(1)}, u32[]{:S(2)}, u32[]{:S(2)}) collective-permute-start(bf16[32,2048]{1,0:T(8,128)(2,1)S(1)} %get-tuple-element.59), channel_id=1, source_target_pairs={{0,48},{1,49},{2,50},{3,51},{4,52},{5,53},{6,54},{7,55},{8,56},{9,... | collective-permute-start | bytes 393224 | tf_op jit(solution)/shard_map/ppermute | solution.py:31
  116.8 22.9 %collective-permute-start.16 = (bf16[32,2048]{1,0:T(8,128)(2,1)S(1)}, bf16[32,2048]{1,0:T(8,128)(2,1)S(1)}, u32[]{:S(2)}, u32[]{:S(2)}) collective-permute-start(bf16[32,2048]{1,0:T(8,128)(2,1)S(1)} %get-tuple-element.60), channel_id=1, source_target_pairs={{0,40},{1,41},{2,42},{3,43},{4,44},{5,45},{6,46},{7,47},{8,48},{9,... | collective-permute-start | bytes 393224 | tf_op jit(solution)/shard_map/ppermute | solution.py:31
  120.7 19.3 %collective-permute-start.12 = (bf16[32,2048]{1,0:T(8,128)(2,1)S(1)}, bf16[32,2048]{1,0:T(8,128)(2,1)S(1)}, u32[]{:S(2)}, u32[]{:S(2)}) collective-permute-start(bf16[32,2048]{1,0:T(8,128)(2,1)S(1)} %get-tuple-element.56), channel_id=1, source_target_pairs={{0,32},{1,33},{2,34},{3,35},{4,36},{5,37},{6,38},{7,39},{8,40},{9,... | collective-permute-start | bytes 393224 | tf_op jit(solution)/shard_map/ppermute | solution.py:31
  122.7 17.4 %collective-permute-start.13 = (bf16[32,2048]{1,0:T(8,128)(2,1)S(1)}, bf16[32,2048]{1,0:T(8,128)(2,1)S(1)}, u32[]{:S(2)}, u32[]{:S(2)}) collective-permute-start(bf16[32,2048]{1,0:T(8,128)(2,1)S(1)} %get-tuple-element.57), channel_id=1, source_target_pairs={{0,56},{1,57},{2,58},{3,59},{4,60},{5,61},{6,62},{7,63},{8,32},{9,... | collective-permute-start | bytes 393224 | tf_op jit(solution)/shard_map/ppermute | solution.py:31
